TPU v7x, 512 devices: a whole 4x8x8 slice. The times are simulated.
512 devices in a mesh: team: 8 (over z), blk: 16 (over y_hi, x), head: 4 (over y_lo, core).
Axes of the slice: x: 4, y: 8 (y_hi: 4, y_lo: 2; y = y_hi * 2 + y_lo), z: 8, core: 2. Of those that a mesh axis runs over, the one named last changes fastest.
Arguments:
- queries: bfloat16 [4096, 8, 8, 128], P('blk', 'head', 'team'), may hold values from -40 to 40
- features: bfloat16 [4096, 8192], P('blk', ('team', 'head')), may hold values from -6 to 6
- adapter_down: bfloat16 [4, 8192, 64], P(None, ('team', 'head')), may hold values from -0.0625 to 0.0625
- adapter_key_up: bfloat16 [4, 64, 8, 128], P(None, None, 'head'), may hold values from -0.75 to 0.75
- adapter_value_up: bfloat16 [4, 64, 8, 128], P(None, None, 'head'), may hold values from -0.75 to 0.75
- base_key: bfloat16 [4096, 8, 128], P('blk', 'head'), may hold values from -6 to 6
- base_value: bfloat16 [4096, 8, 128], P('blk', 'head'), may hold values from -24 to 24
- prefix_key: bfloat16 [8192, 8, 128], P('blk', 'head'), may hold values from -7 to 7
- prefix_value: bfloat16 [8192, 8, 128], P('blk', 'head'), may hold values from -24 to 24
- adapter_ids: int32 [16], replicated, may hold values from 0 to 3
- block_order: int32 [16], replicated, may hold values from 0 to 63
Outputs:
- attended: bfloat16 [4096, 8, 8, 128], P('blk', 'head', 'team')
All inputs are finite; a program needn't handle non-finite values.
Results may differ from a plain program's by a relative error of at most 0.011.
Values may be sent and summed in bfloat16 or wider, within the bound.
A program may use at most 64 MiB of HBM per device.

v0:
```python
import math

import jax
import jax.numpy as jnp
from jax import lax
from jax.sharding import PartitionSpec as P

NEG_FILL = -1e30


def sent_to_all(shard, axis):
    copies = jnp.broadcast_to(shard, (lax.axis_size(axis), *shard.shape))
    return lax.all_to_all(copies, axis, split_axis=0, concat_axis=0, tiled=True)


def taken_together(shard, axis):
    everything = sent_to_all(shard, axis)
    return jnp.sum(everything, axis=0)


def sent_together(arrays, axis, dim, along):
    widths = [a.shape[along] for a in arrays]
    both = jnp.concatenate(arrays, axis=along)
    result = lax.all_gather(both, axis, axis=dim, tiled=True)
    return tuple(jnp.split(result, [sum(widths[:k]) for k in range(1, len(widths))], axis=along))


def block_length(row_count):
    for candidate in range(min(row_count, 1024), 0, -1):
        if row_count % candidate == 0:
            return candidate
    return row_count


def key_positions(row_count, shard_rows, prefix_dev, query_dev, block_order, block_count):
    row_index = jnp.arange(row_count, dtype=jnp.int32)
    holder = row_index // shard_rows
    within = row_index - holder * shard_rows
    block_ids = jnp.arange(block_count, dtype=jnp.int32)
    holder_order = jnp.sum(
        jnp.where(holder[:, None] == block_ids[None, :], block_order[None, :], 0), axis=1
    )
    later = prefix_dev * block_count + holder_order * query_dev + within - prefix_dev
    return jnp.where(within < prefix_dev, holder * prefix_dev + within, later)


def attend(running, query_rows, query_pos, key_rows, value_rows, key_pos):
    row_count = key_rows.shape[0]
    block_rows = block_length(row_count)
    key_blocks = row_count // block_rows
    kv_heads = key_rows.shape[1]
    head_dim = key_rows.shape[2]
    score_scale = 1.0 / math.sqrt(head_dim)
    latest = jnp.max(query_pos)
    key_split = key_rows.reshape((key_blocks, block_rows, kv_heads, head_dim))
    value_split = value_rows.reshape((key_blocks, block_rows, kv_heads, head_dim))
    pos_split = key_pos.reshape((key_blocks, block_rows))

    def advance(carried, block_data):
        block_keys, block_values, block_pos = block_data

        def compute(previous):
            row_max, row_sum, weighted = previous
            scores = (
                jnp.einsum(
                    "tkgd,skd->kgts", query_rows, block_keys, preferred_element_type=jnp.float32
                )
                * score_scale
            )
            visible = block_pos[None, None, None, :] <= query_pos[None, None, :, None]
            scores = jnp.where(visible, scores, NEG_FILL)
            new_max = jnp.maximum(row_max, jnp.max(scores, axis=-1))
            weights = jnp.where(visible, jnp.exp(scores - new_max[..., None]), 0.0)
            factor = jnp.exp(row_max - new_max)
            row_sum = row_sum * factor + jnp.sum(weights, axis=-1)
            product = jnp.einsum(
                "kgts,skd->kgtd",
                weights.astype(jnp.bfloat16),
                block_values,
                preferred_element_type=jnp.float32,
            )
            weighted = weighted * factor[..., None] + product
            return (new_max, row_sum, weighted)

        return (lax.cond(jnp.min(block_pos) > latest, lambda kept: kept, compute, carried), None)

    result, _ = lax.scan(advance, running, (key_split, value_split, pos_split))
    return result


def on_device(
    queries,
    features,
    adapter_down,
    adapter_key_up,
    adapter_value_up,
    base_key,
    base_value,
    prefix_key,
    prefix_value,
    adapter_ids,
    block_order,
):
    block_count = lax.axis_size("blk")
    my_block = lax.axis_index("blk")
    query_dev = queries.shape[0]
    kv_heads = queries.shape[1]
    group_dev = queries.shape[2]
    head_dim = queries.shape[3]
    prefix_dev = prefix_key.shape[0]
    rank_width = adapter_down.shape[2]
    shard_rows = prefix_dev + query_dev
    chosen = adapter_ids[my_block]
    down_rows = lax.dynamic_index_in_dim(adapter_down, chosen, 0, keepdims=False)
    partial_latent = jnp.dot(features, down_rows, preferred_element_type=jnp.float32)
    latent = taken_together(partial_latent, ("team", "head")).astype(jnp.bfloat16)

    def expand(up_table, base_rows):
        up_rows = lax.dynamic_index_in_dim(up_table, chosen, 0, keepdims=False).reshape(
            rank_width, kv_heads * head_dim
        )
        delta = jnp.dot(latent, up_rows, preferred_element_type=jnp.float32).reshape(
            query_dev, kv_heads, head_dim
        )
        return (base_rows.astype(jnp.float32) + delta).astype(jnp.bfloat16)

    key_rows = jnp.concatenate([prefix_key, expand(adapter_key_up, base_key)], axis=0)
    value_rows = jnp.concatenate([prefix_value, expand(adapter_value_up, base_value)], axis=0)
    prefix_total = prefix_dev * block_count
    offsets = jnp.arange(query_dev, dtype=jnp.int32)
    query_pos = prefix_total + block_order[my_block] * query_dev + offsets
    initial = (
        jnp.full((kv_heads, group_dev, query_dev), NEG_FILL, jnp.float32),
        jnp.zeros((kv_heads, group_dev, query_dev), jnp.float32),
        jnp.zeros((kv_heads, group_dev, query_dev, head_dim), jnp.float32),
    )
    key_piece, value_piece = sent_together((key_rows, value_rows), "blk", 0, 1)
    piece_pos = key_positions(
        key_piece.shape[0], shard_rows, prefix_dev, query_dev, block_order, block_count
    )
    row_max, row_sum, weighted = attend(
        initial, queries, query_pos, key_piece, value_piece, piece_pos
    )
    result = weighted / row_sum[..., None]
    return result.transpose(2, 0, 1, 3).astype(jnp.bfloat16)


def solution(mesh):
    placed = (
        P("blk", "head", "team", None),
        P("blk", ("team", "head")),
        P(None, ("team", "head"), None),
        P(None, None, "head", None),
        P(None, None, "head", None),
        P("blk", "head", None),
        P("blk", "head", None),
        P("blk", "head", None),
        P("blk", "head", None),
        P(),
        P(),
    )
    return jax.shard_map(
        on_device,
        mesh=mesh,
        in_specs=placed,
        out_specs=P("blk", "head", "team", None),
        check_vma=False,
    )
```

profile of v0, /device:TPU:1, one launch (start us, length us, event | category | flops | bytes accessed | tf_op | source)
XLA Modules:
  0.0 342.4 jit_solution(14590814455374040289)
XLA Ops:
  6.5 1.3 dynamic_slice.39
  9.7 0.9 convolution_bitcast_fusion.1
  10.6 1.6 broadcast_in_dim.61
  12.2 13.1 %all-to-all-start = ((f32[32,256,64]{1,2,0:T(8,128)}), f32[32,256,64]{1,2,0:T(8,128)S(1)}, u32[]{:S(2)}, u32[]{:S(2)}) async-start(f32[32,256,64]{1,2,0:T(8,128)} %broadcast_in_dim.61), calls=%async_computation | async-start | bytes 4194304 | tf_op jit(solution)/shard_map/all_to_all | solution.py:13
  25.5 0.8 constant_dynamic-slice_fusion.1
  26.4 53.5 %all-to-all-done = f32[32,256,64]{1,2,0:T(8,128)S(1)} async-done(((f32[32,256,64]{1,2,0:T(8,128)}), f32[32,256,64]{1,2,0:T(8,128)S(1)}, u32[]{:S(2)}, u32[]{:S(2)}) %all-to-all-start) | async-done | bytes 2097184 | tf_op jit(solution)/shard_map/all_to_all | solution.py:13
  80.4 1.0 maximum_maximum_fusion
  83.8 163.0 %all-gather.2.cloned.1.call-done = bf16[12288,4,128]{2,0,1:T(8,128)(2,1)} async-done(((bf16[768,4,128]{2,0,1:T(8,128)(2,1)}), bf16[12288,4,128]{2,0,1:T(8,128)(2,1)}) %all-gather.2.cloned.1.call-update) | async-done | bytes 12582928 | tf_op jit(solution)/shard_map/all_gather | solution.py:24
  246.8 5.2 %fusion.46 = (bf16[12288,2,128]{2,0,1:T(8,128)(2,1)S(1)}, bf16[12288,2,128]{2,0,1:T(8,128)(2,1)S(1)}) fusion(bf16[12288,4,128]{2,0,1:T(8,128)(2,1)} %all-gather.2.cloned.1.call-done), kind=kLoop, calls=%fused_computation.76 | loop fusion | bytes 25165824 | tf_op jit(solution)/shard_map/split | solution.py:25
  252.0 3.1 copy.65
  255.1 3.1 copy.67
  258.2 76.4 %while.15 = (s32[]{:T(128)}, f32[2,1,256]{2,0,1:T(2,128)S(1)}, f32[2,1,256]{2,0,1:T(2,128)S(1)}, f32[2,1,256,128]{3,2,0,1:T(8,128)S(1)}, s32[12,1024]{1,0:T(8,12...) while((s32[]{:T(128)}, f32[2,1,256]{2,0,1:T(2,128)S(1)}, ...), condition=%wide.region_9.10_spmd.clone, body=%wide.region_3.9_spmd.clone.sunk | while | flops 275647232 | bytes 9094407 | solution.py:87
  260.2 4.3 %conditional.3 = (f32[2,1,256]{2,0,1:T(2,128)S(1)}, f32[2,1,256]{2,0,1:T(2,128)S(1)}, f32[2,1,256,128]{3,2,0,1:T(8,128)S(1)}) conditional(s32[]{:T(128)} %convert_element_type.57, (s32[1,1024]{1,0:T(1,128)S(1)}, s32[]{:T(128)}, bf16[12,1024,2,128]{3,1,2,0:T(8,128)(2,1)}, s32[]{:T(128)}, bf16[256,2,1,128]{3,0,1,2:T(8,128)(2,1)S(1)}, ...), branch_computations={%region_5.7_spmd, %region_8.8_spmd} | conditional | flops 275646208 | bytes 9080860 | solution.py:85
  260.4 1.5 fusion.2
  262.6 2.0 fusion.5
  266.6 4.3 %conditional.3 = (f32[2,1,256]{2,0,1:T(2,128)S(1)}, f32[2,1,256]{2,0,1:T(2,128)S(1)}, f32[2,1,256,128]{3,2,0,1:T(8,128)S(1)}) conditional(s32[]{:T(128)} %convert_element_type.57, (s32[1,1024]{1,0:T(1,128)S(1)}, s32[]{:T(128)}, bf16[12,1024,2,128]{3,1,2,0:T(8,128)(2,1)}, s32[]{:T(128)}, bf16[256,2,1,128]{3,0,1,2:T(8,128)(2,1)S(1)}, ...), branch_computations={%region_5.7_spmd, %region_8.8_spmd} | conditional | flops 275646208 | bytes 9080860 | solution.py:85
  266.8 1.5 fusion.2
  268.9 2.0 fusion.5
  272.9 4.3 %conditional.3 = (f32[2,1,256]{2,0,1:T(2,128)S(1)}, f32[2,1,256]{2,0,1:T(2,128)S(1)}, f32[2,1,256,128]{3,2,0,1:T(8,128)S(1)}) conditional(s32[]{:T(128)} %convert_element_type.57, (s32[1,1024]{1,0:T(1,128)S(1)}, s32[]{:T(128)}, bf16[12,1024,2,128]{3,1,2,0:T(8,128)(2,1)}, s32[]{:T(128)}, bf16[256,2,1,128]{3,0,1,2:T(8,128)(2,1)S(1)}, ...), branch_computations={%region_5.7_spmd, %region_8.8_spmd} | conditional | flops 275646208 | bytes 9080860 | solution.py:85
  273.2 1.5 fusion.2
  275.3 2.0 fusion.5
  279.3 4.3 %conditional.3 = (f32[2,1,256]{2,0,1:T(2,128)S(1)}, f32[2,1,256]{2,0,1:T(2,128)S(1)}, f32[2,1,256,128]{3,2,0,1:T(8,128)S(1)}) conditional(s32[]{:T(128)} %convert_element_type.57, (s32[1,1024]{1,0:T(1,128)S(1)}, s32[]{:T(128)}, bf16[12,1024,2,128]{3,1,2,0:T(8,128)(2,1)}, s32[]{:T(128)}, bf16[256,2,1,128]{3,0,1,2:T(8,128)(2,1)S(1)}, ...), branch_computations={%region_5.7_spmd, %region_8.8_spmd} | conditional | flops 275646208 | bytes 9080860 | solution.py:85
  279.6 1.5 fusion.2
  281.7 2.0 fusion.5
  285.7 4.3 %conditional.3 = (f32[2,1,256]{2,0,1:T(2,128)S(1)}, f32[2,1,256]{2,0,1:T(2,128)S(1)}, f32[2,1,256,128]{3,2,0,1:T(8,128)S(1)}) conditional(s32[]{:T(128)} %convert_element_type.57, (s32[1,1024]{1,0:T(1,128)S(1)}, s32[]{:T(128)}, bf16[12,1024,2,128]{3,1,2,0:T(8,128)(2,1)}, s32[]{:T(128)}, bf16[256,2,1,128]{3,0,1,2:T(8,128)(2,1)S(1)}, ...), branch_computations={%region_5.7_spmd, %region_8.8_spmd} | conditional | flops 275646208 | bytes 9080860 | solution.py:85
  285.9 1.5 fusion.2
  288.0 2.0 fusion.5
  292.1 4.3 %conditional.3 = (f32[2,1,256]{2,0,1:T(2,128)S(1)}, f32[2,1,256]{2,0,1:T(2,128)S(1)}, f32[2,1,256,128]{3,2,0,1:T(8,128)S(1)}) conditional(s32[]{:T(128)} %convert_element_type.57, (s32[1,1024]{1,0:T(1,128)S(1)}, s32[]{:T(128)}, bf16[12,1024,2,128]{3,1,2,0:T(8,128)(2,1)}, s32[]{:T(128)}, bf16[256,2,1,128]{3,0,1,2:T(8,128)(2,1)S(1)}, ...), branch_computations={%region_5.7_spmd, %region_8.8_spmd} | conditional | flops 275646208 | bytes 9080860 | solution.py:85
  292.3 1.5 fusion.2
  294.4 2.0 fusion.5
  298.4 4.3 %conditional.3 = (f32[2,1,256]{2,0,1:T(2,128)S(1)}, f32[2,1,256]{2,0,1:T(2,128)S(1)}, f32[2,1,256,128]{3,2,0,1:T(8,128)S(1)}) conditional(s32[]{:T(128)} %convert_element_type.57, (s32[1,1024]{1,0:T(1,128)S(1)}, s32[]{:T(128)}, bf16[12,1024,2,128]{3,1,2,0:T(8,128)(2,1)}, s32[]{:T(128)}, bf16[256,2,1,128]{3,0,1,2:T(8,128)(2,1)S(1)}, ...), branch_computations={%region_5.7_spmd, %region_8.8_spmd} | conditional | flops 275646208 | bytes 9080860 | solution.py:85
  298.7 1.5 fusion.2
  300.8 2.0 fusion.5
  304.8 4.3 %conditional.3 = (f32[2,1,256]{2,0,1:T(2,128)S(1)}, f32[2,1,256]{2,0,1:T(2,128)S(1)}, f32[2,1,256,128]{3,2,0,1:T(8,128)S(1)}) conditional(s32[]{:T(128)} %convert_element_type.57, (s32[1,1024]{1,0:T(1,128)S(1)}, s32[]{:T(128)}, bf16[12,1024,2,128]{3,1,2,0:T(8,128)(2,1)}, s32[]{:T(128)}, bf16[256,2,1,128]{3,0,1,2:T(8,128)(2,1)S(1)}, ...), branch_computations={%region_5.7_spmd, %region_8.8_spmd} | conditional | flops 275646208 | bytes 9080860 | solution.py:85
  305.0 1.5 fusion.2
  307.1 2.0 fusion.5
  311.2 4.3 %conditional.3 = (f32[2,1,256]{2,0,1:T(2,128)S(1)}, f32[2,1,256]{2,0,1:T(2,128)S(1)}, f32[2,1,256,128]{3,2,0,1:T(8,128)S(1)}) conditional(s32[]{:T(128)} %convert_element_type.57, (s32[1,1024]{1,0:T(1,128)S(1)}, s32[]{:T(128)}, bf16[12,1024,2,128]{3,1,2,0:T(8,128)(2,1)}, s32[]{:T(128)}, bf16[256,2,1,128]{3,0,1,2:T(8,128)(2,1)S(1)}, ...), branch_computations={%region_5.7_spmd, %region_8.8_spmd} | conditional | flops 275646208 | bytes 9080860 | solution.py:85
  311.4 1.5 fusion.2
  313.5 2.0 fusion.5
  317.5 4.3 %conditional.3 = (f32[2,1,256]{2,0,1:T(2,128)S(1)}, f32[2,1,256]{2,0,1:T(2,128)S(1)}, f32[2,1,256,128]{3,2,0,1:T(8,128)S(1)}) conditional(s32[]{:T(128)} %convert_element_type.57, (s32[1,1024]{1,0:T(1,128)S(1)}, s32[]{:T(128)}, bf16[12,1024,2,128]{3,1,2,0:T(8,128)(2,1)}, s32[]{:T(128)}, bf16[256,2,1,128]{3,0,1,2:T(8,128)(2,1)S(1)}, ...), branch_computations={%region_5.7_spmd, %region_8.8_spmd} | conditional | flops 275646208 | bytes 9080860 | solution.py:85
  317.8 1.5 fusion.2
  319.9 2.0 fusion.5
  323.9 4.3 %conditional.3 = (f32[2,1,256]{2,0,1:T(2,128)S(1)}, f32[2,1,256]{2,0,1:T(2,128)S(1)}, f32[2,1,256,128]{3,2,0,1:T(8,128)S(1)}) conditional(s32[]{:T(128)} %convert_element_type.57, (s32[1,1024]{1,0:T(1,128)S(1)}, s32[]{:T(128)}, bf16[12,1024,2,128]{3,1,2,0:T(8,128)(2,1)}, s32[]{:T(128)}, bf16[256,2,1,128]{3,0,1,2:T(8,128)(2,1)S(1)}, ...), branch_computations={%region_5.7_spmd, %region_8.8_spmd} | conditional | flops 275646208 | bytes 9080860 | solution.py:85
  324.2 1.5 fusion.2
  326.3 2.0 fusion.5
  330.3 4.3 %conditional.3 = (f32[2,1,256]{2,0,1:T(2,128)S(1)}, f32[2,1,256]{2,0,1:T(2,128)S(1)}, f32[2,1,256,128]{3,2,0,1:T(8,128)S(1)}) conditional(s32[]{:T(128)} %convert_element_type.57, (s32[1,1024]{1,0:T(1,128)S(1)}, s32[]{:T(128)}, bf16[12,1024,2,128]{3,1,2,0:T(8,128)(2,1)}, s32[]{:T(128)}, bf16[256,2,1,128]{3,0,1,2:T(8,128)(2,1)S(1)}, ...), branch_computations={%region_5.7_spmd, %region_8.8_spmd} | conditional | flops 275646208 | bytes 9080860 | solution.py:85
  330.5 1.5 fusion.2
  332.6 2.0 fusion.5
  (130 shorter events, 21.2 us)
Async XLA Ops:
  6.5 3.1 copy-start
  12.2 13.2 %copy-start.1 = (bf16[512,2,128]{2,1,0:T(2,128)(2,1)S(1)}, bf16[512,2,128]{2,1,0:T(2,128)(2,1)}, u32[]{:S(2)}) copy-start(bf16[512,2,128]{2,1,0:T(2,128)(2,1)} %param.22) | copy-start | bytes 786436
  12.2 13.3 %copy-start.2 = (bf16[512,2,128]{2,1,0:T(2,128)(2,1)S(1)}, bf16[512,2,128]{2,1,0:T(2,128)(2,1)}, u32[]{:S(2)}) copy-start(bf16[512,2,128]{2,1,0:T(2,128)(2,1)} %param.23) | copy-start | bytes 786436
  12.2 67.6 %all-to-all-start = ((f32[32,256,64]{1,2,0:T(8,128)}), f32[32,256,64]{1,2,0:T(8,128)S(1)}, u32[]{:S(2)}, u32[]{:S(2)}) async-start(f32[32,256,64]{1,2,0:T(8,128)} %broadcast_in_dim.61), calls=%async_computation | async-start | bytes 4194304 | tf_op jit(solution)/shard_map/all_to_all | solution.py:13
  25.3 54.6 %copy-start.3 = (bf16[256,2,128]{2,1,0:T(2,128)(2,1)S(1)}, bf16[256,2,128]{2,1,0:T(2,128)(2,1)}, u32[]{:S(2)}) copy-start(bf16[256,2,128]{2,1,0:T(2,128)(2,1)} %param.20) | copy-start | bytes 393220
  25.3 54.8 %copy-start.4 = (bf16[256,2,128]{2,1,0:T(2,128)(2,1)S(1)}, bf16[256,2,128]{2,1,0:T(2,128)(2,1)}, u32[]{:S(2)}) copy-start(bf16[256,2,128]{2,1,0:T(2,128)(2,1)} %param.21) | copy-start | bytes 393220
  25.4 221.4 %all-gather.2.cloned.1.call-start = ((), (), s32[]{:S(2)}) async-start(), calls=%async_computation.1 | async-start | bytes 13369344 | tf_op jit(solution)/shard_map/all_gather | solution.py:24
  26.3 55.1 %copy-start.6 = (s32[16]{0:T(128)S(1)}, s32[16]{0:T(128)}, u32[]{:S(2)}) copy-start(s32[16]{0:T(128)} %param.25) | copy-start | bytes 196
  79.9 3.7 %copy-start.5 = (bf16[256,2,1,128]{3,1,2,0:T(2,128)(2,1)S(1)}, bf16[256,2,1,128]{3,1,2,0:T(2,128)(2,1)}, u32[]{:S(2)}) copy-start(bf16[256,2,1,128]{3,1,2,0:T(2,128)(2,1)} %param.15) | copy-start | bytes 393220
Sparse Core Ops, SparseCore 0:
  81.5 165.1 all-gather.1
where the time goes:
time: 344 us; the launch traced here: 342 us
  waiting for transfers between devices  216 us (63%)
  matrix products  43.2 us (13%)
  other arithmetic  20.1 us (6%)
  local copies, waits for them, and re-layouts  16.7 us (5%)
  loops' own time  16.7 us (5%)
  between operations  16.1 us (5%)
  starting transfers between devices  13.2 us (4%)
    all_gather x1, waiting for transfers between devices, sent_together(): result = lax.all_gather(both, axis, axis=dim, tiled=True)  163 us
    all_to_all x1, waiting for transfers between devices, sent_to_all(): return lax.all_to_all(copies, axis, split_axis=0, concat_axis=0, tiled=True)  53.5 us
    dot_general x12, matrix products, compute(): jnp.einsum('kgts,skd->kgtd', weights.astype(jnp.bfloat16), block_values,...  23.8 us
    dot_general x12, matrix products, compute(): jnp.einsum('tkgd,skd->kgts', query_rows, block_keys, preferred_element_ty...  18.1 us
    another operation x1, loops' own time, attend(): result, _ = lax.scan(advance, running, (key_split, value_split, pos_split))  16.1 us
    all_to_all x1, starting transfers between devices, sent_to_all(): return lax.all_to_all(copies, axis, split_axis=0, concat_axis=0, tiled=True)  13.1 us
    reduce_min x12, other arithmetic, advance(): jnp.min(block_pos) > latest  8.19 us
  transfers between devices with their start and end apart: 2, of which 2 were waited for; matrix products, arithmetic and copies ran while one was open for 1% of the time, Pallas kernels for 0%

commit v1 on v0

v1 whole, which is shorter than its diff:
```python
import math

import jax
import jax.numpy as jnp
from jax import lax
from jax.experimental import pallas as pl
from jax.experimental.pallas import tpu as pltpu
from jax.sharding import PartitionSpec as P

MESH = pl.DeviceIdType.MESH
BF16 = jnp.bfloat16
F32 = jnp.float32

TEAM, XN, YN, HEADS = 8, 4, 4, 4
QN, HD, KV = 256, 128, 2
PRE, NEW = 64, 32
RANK = 64
LOG_SCALE = math.log2(math.e) / math.sqrt(HD)
FAR = 7
TAIL = 16
MSG = HD + TAIL
NT = (((1,), (1,)), ((), ()))


def spread(ref, rows, count):
    ref[0 : 2 * count, :] = rows.astype(F32)
    return [ref[pl.ds(head, count, stride=2), :] for head in range(KV)]


def kernel(
    ids_ref, order_ref, q_ref, feat_ref, down_ref, kup_ref, vup_ref, bk_ref, bv_ref, pk_ref, pv_ref,
    out_ref,
    stage, stage_base, wide, ups, base, lat_own, lat_recv, lat_sum, qbuf, kvp, kvn, vt, bias,
    scores_r, scores_l, sent, landed, local_sem, send_sem, recv_sem,
):
    team = lax.axis_index("team")
    blk = lax.axis_index("blk")
    head = lax.axis_index("head")
    yh, x = blk // XN, blk % XN

    def at_z(d):
        return {"team": (team + d + TEAM) % TEAM}

    def at_y(d):
        return {"blk": ((yh + d + YN) % YN) * XN + x}

    def at_x(d):
        return {"blk": yh * XN + (x + d + XN) % XN}

    def at_head(d):
        return {"head": (head + d) % HEADS}

    barrier = pltpu.get_barrier_semaphore()
    peers = (
        [at_z(d) for d in range(1, TEAM)]
        + [at_y(d) for d in range(1, YN)]
        + [at_x(1), at_x(-1)]
        + [at_head(d) for d in range(1, HEADS)]
    )
    for peer in peers:
        pl.semaphore_signal(barrier, inc=1, device_id=peer, device_id_type=MESH)

    used = [0]
    started = []

    def copy_to(src, dst, peer):
        index = used[0]
        used[0] += 1
        started.append(
            pltpu.make_async_remote_copy(
                src_ref=src, dst_ref=dst, send_sem=send_sem.at[index], recv_sem=recv_sem.at[index],
                device_id=peer, device_id_type=MESH,
            )
        )
        started[-1].start()
        return started[-1]

    prefix_rows = pl.ds(pl.multiple_of(team * (KV * PRE), KV * PRE), KV * PRE)
    base_rows = pl.ds(pl.multiple_of(team * (KV * NEW), KV * NEW), KV * NEW)
    local = [
        pltpu.make_async_copy(pk_ref.at[prefix_rows], stage.at[0], local_sem.at[0]),
        pltpu.make_async_copy(pv_ref.at[prefix_rows], stage.at[1], local_sem.at[1]),
        pltpu.make_async_copy(bk_ref.at[base_rows], stage_base.at[0], local_sem.at[2]),
        pltpu.make_async_copy(bv_ref.at[base_rows], stage_base.at[1], local_sem.at[3]),
    ]
    for copy in local:
        copy.start()

    chosen = ids_ref[blk]
    down = down_ref[chosen]
    partial = lax.dot_general(
        feat_ref[...], jnp.concatenate([down, down], axis=0), NT, preferred_element_type=F32
    )
    first_half = lax.broadcasted_iota(jnp.int32, (16, HD), 1) < RANK
    for member in range(TEAM):
        row = member * NEW
        lat_own[member] = jnp.where(
            first_half, partial[row : row + 16], partial[row + 16 : row + 32]
        )
    for h, rows in enumerate(spread(wide, q_ref[...], QN)):
        qbuf[0, h] = rows.astype(BF16)
    for kind in range(2):
        local[kind].wait()
        for h, rows in enumerate(spread(wide, stage[kind], PRE)):
            kvp[2 * kind + h, 0, 0] = rows.astype(BF16)

    pl.semaphore_wait(barrier, len(peers))

    z_lat = [
        copy_to(lat_own.at[(team + d) % TEAM], lat_recv.at[d], at_z(d)) for d in range(1, TEAM)
    ]

    q_right, q_left = {}, {}

    def send_q(step, h):
        if step:
            q_right[step, h].wait_recv()
        src = step
        dst = FAR if step == 3 else step + 1
        q_right[step + 1, h] = copy_to(qbuf.at[src, h], qbuf.at[dst, h], at_z(1))
        if step:
            q_left[step, 1 - h].wait_recv()
        src = 3 + step if step else 0
        dst = FAR if step == 3 else 4 + step
        q_left[step + 1, 1 - h] = copy_to(qbuf.at[src, 1 - h], qbuf.at[dst, 1 - h], at_z(-1))

    class Rows:
        def __init__(self, buf):
            self.buf = buf
            self.y, self.right, self.left, self.far = {}, {}, {}, {}

        def send_y(self):
            for d in (1, 3, 2):
                self.y[d] = copy_to(self.buf.at[:, 0, 0], self.buf.at[:, 0, d], at_y(d))

        def send_x(self, d):
            if d:
                self.y[d].wait_recv()
            self.right[d] = copy_to(self.buf.at[:, 0, d], self.buf.at[:, 1, d], at_x(1))
            self.left[d] = copy_to(self.buf.at[:, 0, d], self.buf.at[:, 2, d], at_x(-1))

        def pass_x(self, d):
            keys, values = pl.ds(0, 2), pl.ds(2, 2)
            self.right[d].wait_recv()
            self.far[0, d] = copy_to(self.buf.at[keys, 1, d], self.buf.at[keys, 3, d], at_x(1))
            self.left[d].wait_recv()
            self.far[1, d] = copy_to(self.buf.at[values, 2, d], self.buf.at[values, 3, d], at_x(-1))

    prefix, fresh = Rows(kvp), Rows(kvn)

    send_q(0, 1)
    send_q(0, 0)
    prefix.send_x(0)
    prefix.send_y()

    for kind, table in enumerate((kup_ref, vup_ref)):
        for h, rows in enumerate(spread(wide, table[chosen], RANK)):
            ups[2 * kind + h] = jnp.concatenate([rows, rows], axis=0).astype(BF16)
    for kind in range(2):
        local[2 + kind].wait()
        for h, rows in enumerate(spread(wide, stage_base[kind], NEW)):
            base[2 * kind + h] = rows
    token = order_ref[blk] * QN + lax.broadcasted_iota(jnp.int32, (NEW, QN), 1)
    within = team * NEW + lax.broadcasted_iota(jnp.int32, (NEW, QN), 0)
    for column, dx in enumerate((0, 1, -1, 2)):
        for d in range(YN):
            owner = ((yh - d + YN) % YN) * XN + (x - dx + XN) % XN
            hidden = order_ref[owner] * QN + within > token
            bias[pl.ds((column * YN + d) * NEW, NEW), :] = jnp.where(hidden, -1e30, 0.0)
    for h in range(KV):
        vt[h, HD:MSG, :] = jnp.ones((TAIL, TEAM * (PRE + NEW) * 2), BF16)
    is_first = lax.broadcasted_iota(jnp.int32, (TAIL, QN), 0) == 0
    for side in range(2):
        for slot in range(2):
            landed[side, slot, 0:HD, :] = jnp.zeros((HD, QN), BF16)
            landed[side, slot, HD:MSG, :] = jnp.where(is_first, -1e30, 0.0).astype(BF16)

    for copy in z_lat:
        copy.wait_recv()
    total = lat_own[team]
    for d in range(1, TEAM):
        total = total + lat_recv[d]
    lat_sum[0] = total
    head_lat = [copy_to(lat_sum.at[0], lat_sum.at[d], at_head(d)) for d in range(1, HEADS)]

    prefix.pass_x(0)
    send_q(1, 1)
    prefix.send_x(1)
    prefix.send_x(3)

    for copy in head_lat:
        copy.wait_recv()
    latent = lat_sum[0] + lat_sum[1] + lat_sum[2] + lat_sum[3]
    latent = jnp.concatenate(
        [jnp.where(first_half, latent, 0.0), jnp.where(first_half, 0.0, latent)], axis=0
    ).astype(BF16)
    for part in range(2 * KV):
        delta = jnp.dot(latent, ups[part], preferred_element_type=F32)
        kvn[part, 0, 0] = (base[part] + delta).astype(BF16)
    fresh.send_y()
    fresh.send_x(0)

    send_q(1, 0)
    prefix.send_x(2)
    prefix.pass_x(1)
    prefix.pass_x(3)
    send_q(2, 1)
    fresh.pass_x(0)
    fresh.send_x(1)
    fresh.send_x(3)
    send_q(2, 0)
    prefix.pass_x(2)
    fresh.send_x(2)
    send_q(3, 1)
    for d in (1, 3, 2):
        fresh.pass_x(d)
    q_right[3, 0].wait_recv()
    q_left[3, 1].wait_recv()
    q_right[4, 1].wait_recv()
    q_left[4, 0].wait_recv()
    for rows in (prefix, fresh):
        for copy in rows.far.values():
            copy.wait_recv()

    old_keys, new_keys = XN * YN * PRE, XN * YN * NEW
    for h in range(KV):
        vt[h, 0:HD, 0:old_keys] = kvp[KV + h].reshape(old_keys, HD).T
        vt[h, 0:HD, old_keys:] = kvn[KV + h].reshape(new_keys, HD).T

    tile = 256
    old_tiles, new_tiles = old_keys // tile, new_keys // tile

    def attend(slot, h, scores):
        queries = qbuf[slot, h]
        top = jnp.full((8, QN), -jnp.inf, F32)
        for k in range(old_tiles + new_tiles):
            if k < old_tiles:
                keys = kvp[h, k].reshape(tile, HD)
                s = lax.dot_general(keys, queries, NT, preferred_element_type=F32)
            else:
                n = k - old_tiles
                keys = kvn[h, pl.ds(2 * n, 2)].reshape(tile, HD)
                s = lax.dot_general(keys, queries, NT, preferred_element_type=F32)
                s = s + bias[n * tile : (n + 1) * tile, :]
            scores[k * tile : (k + 1) * tile, :] = s
            top = jnp.maximum(top, jnp.max(s.reshape(tile // 8, 8, QN), axis=0))
        top = jnp.max(top, axis=0, keepdims=True) * LOG_SCALE
        top = top.astype(BF16).astype(F32)
        total = jnp.zeros((MSG, QN), F32)
        for k in range(old_tiles + new_tiles):
            p = jnp.exp2(scores[k * tile : (k + 1) * tile, :] * LOG_SCALE - top).astype(BF16)
            total = total + jnp.dot(
                vt[h, :, k * tile : (k + 1) * tile], p, preferred_element_type=F32
            )
        return total[0:HD], total[HD : HD + 1], top

    def merged(mine, message):
        weighted, row_sum, top = mine
        tail = message[HD:MSG, :].astype(F32)
        other_top, other_sum = tail[0:1], tail[1:2] + tail[2:3]
        both = jnp.maximum(top, other_top)
        here, there = jnp.exp2(top - both), jnp.exp2(other_top - both)
        weighted = weighted * here + message[0:HD, :].astype(F32) * there
        return weighted, row_sum * here + other_sum * there, both

    tail_row = lax.broadcasted_iota(jnp.int32, (TAIL, QN), 0)

    def store(ref, state):
        weighted, row_sum, top = state
        ref[0:HD, :] = weighted.astype(BF16)
        high = row_sum.astype(BF16).astype(F32)
        tail = jnp.where(tail_row == 0, top, jnp.where(tail_row == 1, high, row_sum - high))
        ref[HD:MSG, :] = tail.astype(BF16)

    ring = used[0]

    def message(side, step):
        index = ring + side * 7 + step
        return pltpu.make_async_remote_copy(
            src_ref=sent.at[side, step], dst_ref=landed.at[side, step + 2],
            send_sem=send_sem.at[index], recv_sem=recv_sem.at[index],
            device_id=at_z(1 - 2 * side), device_id_type=MESH,
        )

    def advance(step, carry):
        place = (step + 1) // 2
        from_left = jnp.where(place == 0, FAR, 4 - place)
        from_right = jnp.where(place == 0, FAR, 7 - place)
        h = step % 2
        mine_right = attend(from_right, 1 - h, scores_r)
        mine_left = attend(from_left, h, scores_l)

        @pl.when(step >= 2)
        def _():
            message(0, step - 2).wait_recv()
            message(1, step - 2).wait_recv()

        store(sent.at[0, step], merged(mine_right, landed.at[0, step]))
        message(0, step).start()
        store(sent.at[1, step], merged(mine_left, landed.at[1, step]))
        message(1, step).start()
        return carry

    lax.fori_loop(0, 7, advance, 0)

    own = [attend(0, 0, scores_r), attend(0, 1, scores_l)]
    for side in range(2):
        for step in (5, 6):
            message(side, step).wait_recv()
    for h in range(KV):
        state = merged(own[h], landed.at[0, 7 + h])
        weighted, row_sum, _ = merged(state, landed.at[1, 8 - h])
        wide[pl.ds(h, QN, stride=2), :] = (weighted / row_sum).T
    out_ref[...] = wide[0 : KV * QN, :].astype(BF16)

    for copy in started:
        copy.wait_send()

    def finish(step, carry):
        message(0, step).wait_send()
        message(1, step).wait_send()
        return carry

    lax.fori_loop(0, 7, finish, 0)


def on_device(
    queries, features, adapter_down, adapter_key_up, adapter_value_up,
    base_key, base_value, prefix_key, prefix_value, adapter_ids, block_order,
):
    copies = 7 + 3 + 14 + 2 * 19 + 14
    all_keys = XN * YN * (PRE + NEW)
    vmem = pl.BlockSpec(memory_space=pltpu.VMEM)
    smem = pl.BlockSpec(memory_space=pltpu.SMEM)
    hbm = pl.BlockSpec(memory_space=pl.ANY)
    result = pl.pallas_call(
        kernel,
        out_shape=jax.ShapeDtypeStruct((KV * QN, HD), BF16),
        in_specs=[smem, smem, vmem, vmem, vmem, vmem, vmem, hbm, hbm, hbm, hbm],
        out_specs=vmem,
        scratch_shapes=[
            pltpu.VMEM((2, KV * PRE, HD), BF16),
            pltpu.VMEM((2, KV * NEW, HD), BF16),
            pltpu.VMEM((KV * QN, HD), F32),
            pltpu.VMEM((2 * KV, 2 * RANK, HD), BF16),
            pltpu.VMEM((2 * KV, NEW, HD), F32),
            pltpu.VMEM((TEAM, 16, HD), F32),
            pltpu.VMEM((TEAM, 16, HD), F32),
            pltpu.VMEM((HEADS, 16, HD), F32),
            pltpu.VMEM((TEAM, KV, QN, HD), BF16),
            pltpu.VMEM((2 * KV, XN, YN, PRE, HD), BF16),
            pltpu.VMEM((2 * KV, XN, YN, NEW, HD), BF16),
            pltpu.VMEM((KV, MSG, all_keys), BF16),
            pltpu.VMEM((XN * YN * NEW, QN), F32),
            pltpu.VMEM((all_keys, QN), F32),
            pltpu.VMEM((all_keys, QN), F32),
            pltpu.VMEM((2, 7, MSG, QN), BF16),
            pltpu.VMEM((2, 9, MSG, QN), BF16),
            pltpu.SemaphoreType.DMA((4,)),
            pltpu.SemaphoreType.DMA((copies,)),
            pltpu.SemaphoreType.DMA((copies,)),
        ],
        compiler_params=pltpu.CompilerParams(
            collective_id=0, has_side_effects=True, vmem_limit_bytes=40 * 1024 * 1024
        ),
    )(
        adapter_ids,
        block_order,
        queries.reshape(KV * QN, HD),
        features,
        jnp.swapaxes(adapter_down, 1, 2),
        adapter_key_up.reshape(-1, RANK * KV, HD),
        adapter_value_up.reshape(-1, RANK * KV, HD),
        base_key.reshape(-1, HD),
        base_value.reshape(-1, HD),
        prefix_key.reshape(-1, HD),
        prefix_value.reshape(-1, HD),
    )
    return result.reshape(QN, KV, 1, HD)


def solution(mesh):
    placed = (
        P("blk", "head", "team", None),
        P("blk", ("team", "head")),
        P(None, ("team", "head"), None),
        P(None, None, "head", None),
        P(None, None, "head", None),
        P("blk", "head", None),
        P("blk", "head", None),
        P("blk", "head", None),
        P("blk", "head", None),
        P(),
        P(),
    )
    return jax.shard_map(
        on_device,
        mesh=mesh,
        in_specs=placed,
        out_specs=P("blk", "head", "team", None),
        check_vma=False,
    )
```

time: 344 us -> 65.3 us (0.19)
  the two profiles are of different devices: /device:TPU:1 before, /device:TPU:4 now
where the time goes in v1:
time: 65.3 us; the launch traced here: 65 us
  Pallas kernels  55.4 us (85%)
  local copies, waits for them, and re-layouts  9.55 us (15%)
    pallas_call x1, Pallas kernels, on_device(): pl.pallas_call(kernel, out_shape=jax.ShapeDtypeStruct((KV * QN, HD), BF16...  55.4 us
    unnamed x23, local copies, waits for them, and re-layouts  9.55 us

profile of v1, /device:TPU:4, one launch (start us, length us, event | category | flops | bytes accessed | tf_op | source)
XLA Modules:
  0.0 65.0 jit_solution(7476550003761125475)
XLA Ops:
  0.0 0.0 copy-start.9
  0.0 0.0 copy-start.10
  0.0 0.7 %copy-done.9 = s32[16]{0:T(128)S(1)} copy-done((s32[16]{0:T(128)S(1)}, s32[16]{0:T(128)}, u32[]{:S(2)}) %copy-start.9) | copy-done | bytes 88
  0.7 0.0 copy-done.10
  0.7 0.0 copy-start
  0.7 0.9 %copy-done = bf16[512,2,128]{2,1,0:T(2,128)(2,1)S(1)} copy-done((bf16[512,2,128]{2,1,0:T(2,128)(2,1)S(1)}, bf16[512,2,128]{2,1,0:T(2,128)(2,1)}, u32[]{:S(2)}) %copy-start) | copy-done | bytes 262168
  1.6 0.0 copy-start.1
  1.6 0.9 %copy-done.1 = bf16[512,2,128]{2,1,0:T(2,128)(2,1)S(1)} copy-done((bf16[512,2,128]{2,1,0:T(2,128)(2,1)S(1)}, bf16[512,2,128]{2,1,0:T(2,128)(2,1)}, u32[]{:S(2)}) %copy-start.1) | copy-done | bytes 262168
  2.6 0.0 copy-start.2
  2.6 0.9 %copy-done.2 = bf16[256,2,1,128]{3,1,2,0:T(2,128)(2,1)S(1)} copy-done((bf16[256,2,1,128]{3,1,2,0:T(2,128)(2,1)S(1)}, bf16[256,2,1,128]{3,1,2,0:T(2,128)(2,1)}, u32[]{:S(2)}) %copy-start.2) | copy-done | bytes 131096
  3.5 0.0 copy-start.3
  3.5 0.9 %copy-done.3 = bf16[256,256]{1,0:T(8,128)(2,1)S(1)} copy-done((bf16[256,256]{1,0:T(8,128)(2,1)S(1)}, bf16[256,256]{1,0:T(8,128)(2,1)}, u32[]{:S(2)}) %copy-start.3) | copy-done | bytes 131096
  4.4 0.0 copy-start.4
  4.4 0.9 %copy-done.4 = bf16[4,256,64]{1,2,0:T(8,128)(2,1)S(1)} copy-done((bf16[4,256,64]{1,2,0:T(8,128)(2,1)S(1)}, bf16[4,256,64]{1,2,0:T(8,128)(2,1)}, u32[]{:S(2)}) %copy-start.4) | copy-done | bytes 131096
  5.3 0.0 copy-start.5
  5.3 0.9 %copy-done.5 = bf16[4,64,2,128]{3,2,1,0:T(2,128)(2,1)S(1)} copy-done((bf16[4,64,2,128]{3,2,1,0:T(2,128)(2,1)S(1)}, bf16[4,64,2,128]{3,2,1,0:T(2,128)(2,1)}, u32[]{:S(2)}) %copy-start.5) | copy-done | bytes 131096
  6.2 0.0 copy-start.6
  6.2 0.9 %copy-done.6 = bf16[4,64,2,128]{3,2,1,0:T(2,128)(2,1)S(1)} copy-done((bf16[4,64,2,128]{3,2,1,0:T(2,128)(2,1)S(1)}, bf16[4,64,2,128]{3,2,1,0:T(2,128)(2,1)}, u32[]{:S(2)}) %copy-start.6) | copy-done | bytes 131096
  7.1 0.0 copy-start.7
  7.1 0.9 %copy-done.7 = bf16[256,2,128]{2,1,0:T(2,128)(2,1)S(1)} copy-done((bf16[256,2,128]{2,1,0:T(2,128)(2,1)S(1)}, bf16[256,2,128]{2,1,0:T(2,128)(2,1)}, u32[]{:S(2)}) %copy-start.7) | copy-done | bytes 131096
  8.0 0.0 copy-start.8
  8.0 0.9 %copy-done.8 = bf16[256,2,128]{2,1,0:T(2,128)(2,1)S(1)} copy-done((bf16[256,2,128]{2,1,0:T(2,128)(2,1)S(1)}, bf16[256,2,128]{2,1,0:T(2,128)(2,1)}, u32[]{:S(2)}) %copy-start.8) | copy-done | bytes 131096
  8.9 55.4 %shard_map.109 = bf16[512,128]{1,0:T(8,128)(2,1)S(1)} custom-call(s32[16]{0:T(128)S(1)} %copy-done.9, s32[16]{0:T(128)S(1)} %copy-done.10, bf16[512,128]{1,0:T(8,128)(2,1)S(1)} %bitcast.14, bf16[256,256]{1,0:T(8,128)(2,1)S(1)} %copy-done.3, bf16[4,64,256]{2,1,0:T(8,128)(2,1)S(1)} %bitcast.15, bf16[4,128,128]{2,1,0:T(8,128)(2,1)S(1)} %bitcast.16, ...), custom_call_target="tpu_custom_call" | custom-call | tf_op jit(solution)/shard_map/pallas_call | solution.py:336
  64.3 0.7 %copy.14 = bf16[256,2,1,128]{3,1,2,0:T(2,128)(2,1)} copy(bf16[256,2,1,128]{3,1,2,0:T(2,128)(2,1)S(1)} %bitcast.11) | data formatting | bytes 262144
Async XLA Ops:
  0.0 0.7 %copy-start.9 = (s32[16]{0:T(128)S(1)}, s32[16]{0:T(128)}, u32[]{:S(2)}) copy-start(s32[16]{0:T(128)} %ids_ref.1) | copy-start | bytes 196
  0.0 0.7 %copy-start.10 = (s32[16]{0:T(128)S(1)}, s32[16]{0:T(128)}, u32[]{:S(2)}) copy-start(s32[16]{0:T(128)} %order_ref.1) | copy-start | bytes 196
  0.7 0.9 %copy-start = (bf16[512,2,128]{2,1,0:T(2,128)(2,1)S(1)}, bf16[512,2,128]{2,1,0:T(2,128)(2,1)}, u32[]{:S(2)}) copy-start(bf16[512,2,128]{2,1,0:T(2,128)(2,1)} %param.18) | copy-start | bytes 786436
  1.6 0.9 %copy-start.1 = (bf16[512,2,128]{2,1,0:T(2,128)(2,1)S(1)}, bf16[512,2,128]{2,1,0:T(2,128)(2,1)}, u32[]{:S(2)}) copy-start(bf16[512,2,128]{2,1,0:T(2,128)(2,1)} %param.19) | copy-start | bytes 786436
  2.6 0.9 %copy-start.2 = (bf16[256,2,1,128]{3,1,2,0:T(2,128)(2,1)S(1)}, bf16[256,2,1,128]{3,1,2,0:T(2,128)(2,1)}, u32[]{:S(2)}) copy-start(bf16[256,2,1,128]{3,1,2,0:T(2,128)(2,1)} %param.11) | copy-start | bytes 393220
  3.5 0.9 %copy-start.3 = (bf16[256,256]{1,0:T(8,128)(2,1)S(1)}, bf16[256,256]{1,0:T(8,128)(2,1)}, u32[]{:S(2)}) copy-start(bf16[256,256]{1,0:T(8,128)(2,1)} %feat_ref.1) | copy-start | bytes 393220
  4.4 0.9 %copy-start.4 = (bf16[4,256,64]{1,2,0:T(8,128)(2,1)S(1)}, bf16[4,256,64]{1,2,0:T(8,128)(2,1)}, u32[]{:S(2)}) copy-start(bf16[4,256,64]{1,2,0:T(8,128)(2,1)} %param.13) | copy-start | bytes 393220
  5.3 0.9 %copy-start.5 = (bf16[4,64,2,128]{3,2,1,0:T(2,128)(2,1)S(1)}, bf16[4,64,2,128]{3,2,1,0:T(2,128)(2,1)}, u32[]{:S(2)}) copy-start(bf16[4,64,2,128]{3,2,1,0:T(2,128)(2,1)} %param.14) | copy-start | bytes 393220
  6.2 0.9 %copy-start.6 = (bf16[4,64,2,128]{3,2,1,0:T(2,128)(2,1)S(1)}, bf16[4,64,2,128]{3,2,1,0:T(2,128)(2,1)}, u32[]{:S(2)}) copy-start(bf16[4,64,2,128]{3,2,1,0:T(2,128)(2,1)} %param.15) | copy-start | bytes 393220
  7.1 0.9 %copy-start.7 = (bf16[256,2,128]{2,1,0:T(2,128)(2,1)S(1)}, bf16[256,2,128]{2,1,0:T(2,128)(2,1)}, u32[]{:S(2)}) copy-start(bf16[256,2,128]{2,1,0:T(2,128)(2,1)} %param.16) | copy-start | bytes 393220
  8.0 0.9 %copy-start.8 = (bf16[256,2,128]{2,1,0:T(2,128)(2,1)S(1)}, bf16[256,2,128]{2,1,0:T(2,128)(2,1)}, u32[]{:S(2)}) copy-start(bf16[256,2,128]{2,1,0:T(2,128)(2,1)} %param.17) | copy-start | bytes 393220

commit v2 on v0

v2 whole, which is shorter than its diff:
```python
import math

import jax
import jax.numpy as jnp
from jax import lax
from jax.experimental import pallas as pl
from jax.experimental.pallas import tpu as pltpu
from jax.sharding import PartitionSpec as P

MESH = pl.DeviceIdType.MESH
BF16 = jnp.bfloat16
F32 = jnp.float32

TEAM, XN, YN = 8, 4, 4
QN, HD, KV = 256, 128, 2
PRE, NEW = 128, 64
PIECE = 2 * (PRE + NEW)
RANK, ADAPTERS = 64, 4
LOG_SCALE = math.log2(math.e) / math.sqrt(HD)
TAIL = 16
MSG = HD + TAIL
NT = (((1,), (1,)), ((), ()))
DIST = (4, 3, 5, 2, 6, 1, 7, 0)
COLUMNS = (0, 1, -1, 2)
GROUP = 6 * PRE
FIRST = [(0, 0), (1, 0), (2, 0), (3, 0), (0, 1), (0, 3)]
SECOND = [(1, 1), (2, 1), (3, 1), (1, 3), (2, 3), (3, 3)]
LAST = [(0, 2), (1, 2), (2, 2), (3, 2)]


def kernel(
    ids_ref, order_ref, q_hbm, feat_hbm, down_hbm, kup_hbm, vup_hbm, bk_hbm, bv_hbm, pk_hbm, pv_hbm,
    out_ref,
    q_ref, feat_ref, down_ref, up_ref, pre_ref, base_ref, wide, own_rows, ups, lat_part, lat_sib,
    lat_chip, lat_team, lat_pair, lat_all, q_own, qbuf, kv, keys, values, vt, bias, scores_a, scores_b,
    acc, tops, sent, from_sib, landed, local_sem, send_sem, recv_sem, core_send, core_recv, home_send, home_recv,
):
    team = lax.axis_index("team")
    blk = lax.axis_index("blk")
    head = lax.axis_index("head")
    yh, x = blk // XN, blk % XN
    ylo, core = head // 2, head % 2
    half, mine = team // 4, team % 2
    is_owner = (team % 4) // 2 == core
    not_owner = jnp.logical_not(is_owner)

    def at_z(d):
        return {"team": (team + d + TEAM) % TEAM}

    def at_blk(dy, dx):
        return {"blk": ((yh + dy + YN) % YN) * XN + (x + dx + XN) % XN}

    sibling = {"head": ylo * 2 + 1 - core}
    beside = {"head": (1 - ylo) * 2 + core}
    others = [(d, c) for d in range(YN) for c in range(XN) if (d, c) != (0, 0)]

    barrier = pltpu.get_barrier_semaphore()
    peers = [at_z(d) for d in range(1, TEAM)] + [sibling, beside]
    peers += [at_blk(d, COLUMNS[c]) for d, c in others]
    for peer in peers:
        pl.semaphore_signal(barrier, inc=1, device_id=peer, device_id_type=MESH)

    used = [0]

    def link(src, dst, peer):
        index = used[0]
        used[0] += 1
        return pltpu.make_async_remote_copy(
            src_ref=src, dst_ref=dst, send_sem=send_sem.at[index], recv_sem=recv_sem.at[index],
            device_id=peer, device_id_type=MESH,
        )

    pre_rows = pl.ds(pl.multiple_of(half * (KV * 2 * PRE), KV * 2 * PRE), KV * 2 * PRE)
    base_rows = pl.ds(pl.multiple_of(half * (KV * 2 * NEW), KV * 2 * NEW), KV * 2 * NEW)
    pairs = [
        (feat_hbm, feat_ref), (down_hbm, down_ref), (q_hbm, q_ref),
        (pk_hbm.at[pre_rows], pre_ref.at[0]), (pv_hbm.at[pre_rows], pre_ref.at[1]),
        (bk_hbm.at[base_rows], base_ref.at[0]), (bv_hbm.at[base_rows], base_ref.at[1]),
        (kup_hbm, up_ref.at[0]), (vup_hbm, up_ref.at[1]),
    ]
    local = [pltpu.make_async_copy(src, dst, local_sem.at[k]) for k, (src, dst) in enumerate(pairs)]
    for copy in local:
        copy.start()

    for copy in local[:2]:
        copy.wait()
    down = down_ref[ids_ref[blk]]
    partial = lax.dot_general(
        feat_ref[...], jnp.concatenate([down, down], axis=0), NT, preferred_element_type=F32
    )
    first_half = lax.broadcasted_iota(jnp.int32, (32, HD), 1) < RANK
    for quarter in range(4):
        row = quarter * NEW
        lat_part[quarter % 2, quarter // 2] = jnp.where(
            first_half, partial[row : row + 32], partial[row + 32 : row + 64]
        )

    for copy in local[2:]:
        copy.wait()
    wide[0 : KV * QN, :] = q_ref[...].astype(F32)
    for h in range(KV):
        q_own[h] = wide[pl.ds(h, QN, stride=2), :].astype(BF16)

    @pl.when(is_owner)
    def _():
        def pick(rows, count):
            wide[0 : 2 * count, :] = rows.astype(F32)
            even, odd = (wide[pl.ds(h, count, stride=2), :] for h in range(KV))
            return jnp.where(mine == 0, even, odd).astype(BF16)

        for kind in range(2):
            rows = pick(pre_ref[kind], 2 * PRE)
            fresh = pick(base_ref[kind], 2 * NEW)
            for c in range(2):
                own_rows[c, kind * PRE : (kind + 1) * PRE, :] = rows[c * PRE : (c + 1) * PRE]
                at = 2 * PRE + kind * NEW
                own_rows[c, at : at + NEW, :] = fresh[c * NEW : (c + 1) * NEW]
            for a in range(ADAPTERS):
                ups[a, :, kind * HD : (kind + 1) * HD] = pick(up_ref[kind, a], RANK)
        kv[0, 0] = own_rows[core]
        qbuf[7] = q_own[mine]

    pl.semaphore_wait(barrier, len(peers))

    lat_core = link(lat_part.at[1 - core], lat_sib, sibling)
    share_rows = link(own_rows.at[1 - core], kv.at[0, 0], sibling)
    share_ups = link(ups, ups, sibling)
    share_q = [link(qbuf.at[i], qbuf.at[i], sibling) for i in range(TEAM)]
    team_q = [
        link(q_own.at[(team + DIST[i]) % 2], qbuf.at[i], at_z(DIST[i])) for i in range(TEAM - 1)
    ]
    takes_q = [((team + DIST[i]) % 4) // 2 == core for i in range(TEAM - 1)]

    lat_core.start()

    @pl.when(is_owner)
    def _():
        share_rows.start()

    lat_core.wait_recv()
    for h in range(2):
        lat_chip[h] = lat_part[core, h] + lat_sib[h]
    lat_z = [
        link(lat_chip.at[((team + d) % TEAM) // 4], lat_team.at[d], at_z(d)) for d in range(1, TEAM)
    ]
    for copy in lat_z:
        copy.start()
    for i in range(TEAM - 1):
        pl.when(takes_q[i])(team_q[i].start)

    @pl.when(not_owner)
    def _():
        share_rows.wait_recv()

    down_y = {d: link(kv.at[0, 0], kv.at[0, d], at_blk(d, 0)) for d in (1, 3, 2)}
    round_x = {}

    def send_x(d):
        if d:
            down_y[d].wait_recv()
        for c in (1, 2, 3):
            round_x[c, d] = link(kv.at[0, d], kv.at[c, d], at_blk(0, COLUMNS[c]))
            round_x[c, d].start()

    for copy in down_y.values():
        copy.start()
    send_x(0)

    @pl.when(is_owner)
    def _():
        share_ups.start()
        share_q[7].start()

    token = order_ref[blk] * QN + lax.broadcasted_iota(jnp.int32, (NEW, QN), 1)
    within = (2 * half + core) * NEW + lax.broadcasted_iota(jnp.int32, (NEW, QN), 0)

    def owner_of(column, d):
        return ((yh - d + YN) % YN) * XN + (x - COLUMNS[column] + XN) % XN

    for k, (column, d) in enumerate(FIRST + SECOND + LAST):
        hidden = order_ref[owner_of(column, d)] * QN + within > token
        bias[k * NEW : (k + 1) * NEW, :] = jnp.where(hidden, -1e30, 0.0)
    for group in range(4):
        vt[group, HD:MSG, :] = jnp.ones((TAIL, GROUP), BF16)

    send_x(1)
    send_x(3)

    for copy in lat_z:
        copy.wait_recv()
    total = lat_chip[half]
    for d in range(1, TEAM):
        total = total + lat_team[d]
    lat_pair[0] = total
    lat_y = link(lat_pair.at[0], lat_pair.at[1], beside)
    lat_y.start()

    @pl.when(is_owner)
    def _():
        for i in (5, 6, 3, 4, 1, 2, 0):
            team_q[i].wait_recv()
            share_q[i].start()

    lat_y.wait_recv()
    lat_all[0, 0] = (lat_pair[0] + lat_pair[1]).astype(BF16)
    lat_blk = {
        (c, d): link(lat_all.at[0, 0], lat_all.at[c, d], at_blk(d, COLUMNS[c])) for d, c in others
    }
    for copy in lat_blk.values():
        copy.start()

    send_x(2)

    @pl.when(not_owner)
    def _():
        for i in range(TEAM):
            share_q[i].wait_recv()
        share_ups.wait_recv()

    def put_prefix(group, at, slot):
        keys[group, at : at + PRE, :] = kv[slot[0], slot[1], 0:PRE, :]
        values[group, at : at + PRE, :] = kv[slot[0], slot[1], PRE : 2 * PRE, :]

    def put_fresh(group, at, slot):
        packed = lat_all[slot[0], slot[1]].astype(F32)
        latent = jnp.concatenate(
            [jnp.where(first_half, packed, 0.0), jnp.where(first_half, 0.0, packed)], axis=0
        ).astype(BF16)
        up = ups[ids_ref[owner_of(*slot)]]
        delta = jnp.dot(latent, jnp.concatenate([up, up], axis=0), preferred_element_type=F32)
        base = kv[slot[0], slot[1], 2 * PRE : PIECE, :].astype(F32)
        keys[group, at : at + NEW, :] = (base[0:NEW] + delta[:, 0:HD]).astype(BF16)
        values[group, at : at + NEW, :] = (base[NEW:] + delta[:, HD:]).astype(BF16)

    def turn(group):
        vt[group, 0:HD, :] = values[group].T

    def step(group, i, scores):
        s = lax.dot_general(keys[group], qbuf[i], NT, preferred_element_type=F32)
        if group == 2:
            s = s + bias[0:GROUP, :]
        if group == 3:
            plain = 4 * PRE
            s = jnp.concatenate([s[0:plain], s[plain:] + bias[GROUP:, :]], axis=0)
        scores[...] = s
        top = jnp.max(s.reshape(GROUP // 8, 8, QN), axis=0)
        top = jnp.max(top, axis=0, keepdims=True) * LOG_SCALE
        top = top.astype(BF16).astype(F32)
        if group:
            before = tops[i, 0:1, :]
            top = jnp.maximum(top, before)
        p = jnp.exp2(scores[...] * LOG_SCALE - top).astype(BF16)
        weighted = jnp.dot(vt[group], p, preferred_element_type=F32)
        if group:
            weighted = weighted + acc[i] * jnp.exp2(before - top)
        acc[i] = weighted
        tops[i] = jnp.broadcast_to(top, (8, QN))

    def run(group):
        def both(k, carry):
            step(group, 2 * k, scores_a)
            step(group, 2 * k + 1, scores_b)
            return carry

        lax.fori_loop(0, TEAM // 2, both, 0)

    for k, slot in enumerate(FIRST):
        if slot[0]:
            round_x[slot].wait_recv()
        put_prefix(0, k * PRE, slot)
    turn(0)
    run(0)

    for k, slot in enumerate(SECOND):
        round_x[slot].wait_recv()
        put_prefix(1, k * PRE, slot)
    turn(1)
    run(1)

    for copy in lat_blk.values():
        copy.wait_recv()
    for k, slot in enumerate(FIRST + SECOND):
        put_fresh(2, k * NEW, slot)
    turn(2)
    run(2)

    for k, slot in enumerate(LAST):
        if slot[0]:
            round_x[slot].wait_recv()
        put_prefix(3, k * PRE, slot)
        put_fresh(3, 4 * PRE + k * NEW, slot)
    turn(3)

    tail_row = lax.broadcasted_iota(jnp.int32, (TAIL, QN), 0)

    def store(ref, state):
        weighted, row_sum, top = state
        ref[0:HD, :] = weighted.astype(BF16)
        high = row_sum.astype(BF16).astype(F32)
        tail = jnp.where(tail_row == 0, top, jnp.where(tail_row == 1, high, row_sum - high))
        ref[HD:MSG, :] = tail.astype(BF16)

    def held(i):
        return acc[i, 0:HD, :], acc[i, HD : HD + 1, :], tops[i, 0:1, :]

    def read(ref):
        tail = ref[HD:MSG, :].astype(F32)
        return ref[0:HD, :].astype(F32), tail[1:2] + tail[2:3], tail[0:1]

    def merged(one, other):
        top = jnp.maximum(one[2], other[2])
        a, b = jnp.exp2(one[2] - top), jnp.exp2(other[2] - top)
        return one[0] * a + other[0] * b, one[1] * a + other[1] * b, top

    home_slot = mine * 2 + half

    def to_sibling(i):
        return pltpu.make_async_remote_copy(
            src_ref=sent.at[i], dst_ref=from_sib.at[i], send_sem=core_send.at[i], recv_sem=core_recv.at[i],
            device_id=sibling, device_id_type=MESH,
        )

    def homeward(i, slot):
        away = jnp.where(i % 2 == 0, 4 + i // 2, 4 - (i + 1) // 2)
        return pltpu.make_async_remote_copy(
            src_ref=sent.at[i], dst_ref=landed.at[slot], send_sem=home_send.at[i], recv_sem=home_recv.at[slot],
            device_id={"team": (team - away + TEAM) % TEAM}, device_id_type=MESH,
        )

    def merge_and_send(i):
        to_sibling(i).wait_recv()
        store(sent.at[i], merged(held(i), read(from_sib.at[i])))
        homeward(i, home_slot).start()

    def final(k, carry):
        step(3, 2 * k, scores_a)
        step(3, 2 * k + 1, scores_b)

        @pl.when(not_owner)
        def _():
            for i in (2 * k, 2 * k + 1):
                store(sent.at[i], held(i))
                to_sibling(i).start()

        @pl.when(jnp.logical_and(is_owner, k > 0))
        def _():
            for i in (2 * k - 2, 2 * k - 1):
                merge_and_send(i)

        return carry

    lax.fori_loop(0, TEAM // 2, final, 0)

    @pl.when(is_owner)
    def _():
        merge_and_send(6)
        to_sibling(7).wait_recv()
        store(landed.at[home_slot], merged(held(7), read(from_sib.at[7])))

    for h in range(KV):
        for part in range(2):
            slot = h * 2 + part

            @pl.when(team != part * 4 + core * 2 + h)
            def _():
                homeward(0, slot).wait_recv()

        weighted, row_sum, _ = merged(read(landed.at[h * 2]), read(landed.at[h * 2 + 1]))
        wide[pl.ds(h, QN, stride=2), :] = (weighted / row_sum).T
    out_ref[...] = wide[0 : KV * QN, :].astype(BF16)

    for copy in [lat_core, lat_y, *lat_z, *down_y.values(), *round_x.values(), *lat_blk.values()]:
        copy.wait_send()
    for i in range(TEAM - 1):
        pl.when(takes_q[i])(team_q[i].wait_send)

    @pl.when(is_owner)
    def _():
        for copy in [share_rows, share_ups, *share_q]:
            copy.wait_send()

        def gone(i, carry):
            homeward(i, home_slot).wait_send()
            return carry

        lax.fori_loop(0, TEAM - 1, gone, 0)

    @pl.when(not_owner)
    def _():
        def gone(i, carry):
            to_sibling(i).wait_send()
            return carry

        lax.fori_loop(0, TEAM, gone, 0)


def on_device(
    queries, features, adapter_down, adapter_key_up, adapter_value_up,
    base_key, base_value, prefix_key, prefix_value, adapter_ids, block_order,
):
    copies = 1 + 1 + 1 + 8 + 7 + 7 + 1 + 15 + 3 + 12
    vmem = pl.BlockSpec(memory_space=pltpu.VMEM)
    smem = pl.BlockSpec(memory_space=pltpu.SMEM)
    hbm = pl.BlockSpec(memory_space=pl.ANY)
    dma = pltpu.SemaphoreType.DMA
    result = pl.pallas_call(
        kernel,
        out_shape=jax.ShapeDtypeStruct((KV * QN, HD), BF16),
        in_specs=[smem] * 2 + [hbm] * 9,
        out_specs=vmem,
        scratch_shapes=[
            pltpu.VMEM((KV * QN, HD), BF16),
            pltpu.VMEM(features.shape, BF16),
            pltpu.VMEM((ADAPTERS, RANK, features.shape[1]), BF16),
            pltpu.VMEM((2, ADAPTERS, KV * RANK, HD), BF16),
            pltpu.VMEM((2, KV * 2 * PRE, HD), BF16),
            pltpu.VMEM((2, KV * 2 * NEW, HD), BF16),
            pltpu.VMEM((KV * QN, HD), F32),
            pltpu.VMEM((2, PIECE, HD), BF16),
            pltpu.VMEM((ADAPTERS, RANK, 2 * HD), BF16),
            pltpu.VMEM((2, 2, 32, HD), F32),
            pltpu.VMEM((2, 32, HD), F32),
            pltpu.VMEM((2, 32, HD), F32),
            pltpu.VMEM((TEAM, 32, HD), F32),
            pltpu.VMEM((2, 32, HD), F32),
            pltpu.VMEM((XN, YN, 32, HD), BF16),
            pltpu.VMEM((KV, QN, HD), BF16),
            pltpu.VMEM((TEAM, QN, HD), BF16),
            pltpu.VMEM((XN, YN, PIECE, HD), BF16),
            pltpu.VMEM((4, GROUP, HD), BF16),
            pltpu.VMEM((4, GROUP, HD), BF16),
            pltpu.VMEM((4, MSG, GROUP), BF16),
            pltpu.VMEM((XN * YN * NEW, QN), F32),
            pltpu.VMEM((GROUP, QN), F32),
            pltpu.VMEM((GROUP, QN), F32),
            pltpu.VMEM((TEAM, MSG, QN), F32),
            pltpu.VMEM((TEAM, 8, QN), F32),
            pltpu.VMEM((TEAM, MSG, QN), BF16),
            pltpu.VMEM((TEAM, MSG, QN), BF16),
            pltpu.VMEM((4, MSG, QN), BF16),
            dma((9,)),
            dma((copies,)),
            dma((copies,)),
            dma((TEAM,)),
            dma((TEAM,)),
            dma((TEAM,)),
            dma((4,)),
        ],
        compiler_params=pltpu.CompilerParams(
            collective_id=0, has_side_effects=True, vmem_limit_bytes=60 * 1024 * 1024
        ),
    )(
        adapter_ids,
        block_order,
        queries.reshape(KV * QN, HD),
        features,
        jnp.swapaxes(adapter_down, 1, 2),
        adapter_key_up.reshape(-1, RANK * KV, HD),
        adapter_value_up.reshape(-1, RANK * KV, HD),
        base_key.reshape(-1, HD),
        base_value.reshape(-1, HD),
        prefix_key.reshape(-1, HD),
        prefix_value.reshape(-1, HD),
    )
    return result.reshape(QN, KV, 1, HD)


def solution(mesh):
    placed = (
        P("blk", "head", "team", None),
        P("blk", ("team", "head")),
        P(None, ("team", "head"), None),
        P(None, None, "head", None),
        P(None, None, "head", None),
        P("blk", "head", None),
        P("blk", "head", None),
        P("blk", "head", None),
        P("blk", "head", None),
        P(),
        P(),
    )
    return jax.shard_map(
        on_device,
        mesh=mesh,
        in_specs=placed,
        out_specs=P("blk", "head", "team", None),
        check_vma=False,
    )
```

time: 344 us -> 63 us (0.18)
  waiting for transfers between devices: 216 us -> 0 us
  Pallas kernels: 0 us -> 61.1 us
  matrix products: 43.2 us -> 0 us
  other arithmetic: 20.1 us -> 0 us
  loops' own time: 16.7 us -> 0 us
  between operations: 16.1 us -> 0.01 us
  local copies, waits for them, and re-layouts: 16.7 us -> 1.65 us
  starting transfers between devices: 13.2 us -> 0 us
    all_gather x1 -> x0, waiting for transfers between devices: 163 us -> none  [sent_together(): result = lax.all_gather(both, axis, axis=dim, tiled=True)]
    pallas_call x0 -> x1, Pallas kernels: none -> 61.1 us  [on_device(): pl.pallas_call(kernel, out_shape=jax.ShapeDtypeStruct((KV * QN, HD), BF16...]
    all_to_all x1 -> x0, waiting for transfers between devices: 53.5 us -> none  [sent_to_all(): return lax.all_to_all(copies, axis, split_axis=0, concat_axis=0, tiled=True)]
    dot_general x27 -> x0, matrix products: 43.2 us -> none  [the longest x12 23.8 us: compute(): jnp.einsum('kgts,skd->kgtd', weights.astype(jnp.bfloat16), block_values,...]
    another operation x13 -> x0, loops' own time: 16.7 us -> none  [the longest x1 16.1 us: attend(): result, _ = lax.scan(advance, running, (key_split, value_split, pos_split))]
    all_to_all x1 -> x0, starting transfers between devices: 13.1 us -> none  [sent_to_all(): return lax.all_to_all(copies, axis, split_axis=0, concat_axis=0, tiled=True)]
    reduce_min x12 -> x0, other arithmetic: 8.19 us -> none  [advance(): jnp.min(block_pos) > latest]
    reduce_sum x14 -> x0, other arithmetic: 7.13 us -> none  [the longest x12 6.78 us: compute(): row_sum = row_sum * factor + jnp.sum(weights, axis=-1)]
  transfers between devices with their start and end apart: 2 -> 0, of which waited for: 2 -> 0; matrix products, arithmetic and copies ran while one was open for 1% -> 0% of each run, Pallas kernels for 0% -> 0%
where the time goes in v2:
time: 63 us; the launch traced here: 62.8 us
  Pallas kernels  61.1 us (97%)
  local copies, waits for them, and re-layouts  1.65 us (3%)
    pallas_call x1, Pallas kernels, on_device(): pl.pallas_call(kernel, out_shape=jax.ShapeDtypeStruct((KV * QN, HD), BF16...  61.1 us
    unnamed x1, local copies, waits for them, and re-layouts  1.65 us

profile of v2, /device:TPU:1, one launch (start us, length us, event | category | flops | bytes accessed | tf_op | source)
XLA Modules:
  0.0 62.8 jit_solution(4626003278028041702)
XLA Ops:
  0.0 61.1 %shard_map.109 = bf16[512,128]{1,0:T(8,128)(2,1)} custom-call(s32[16]{0:T(128)} %ids_ref.1, s32[16]{0:T(128)} %order_ref.1, bf16[512,128]{1,0:T(8,128)(2,1)} %bitcast.14, bf16[256,256]{1,0:T(8,128)(2,1)} %feat_hbm.1, bf16[4,64,256]{2,1,0:T(8,128)(2,1)} %bitcast.15, bf16[4,128,128]{2,1,0:T(8,128)(2,1)} %bitcast.16, bf16[4,128,128]{2,1,0:T(8,128)(2,1)} %bitcast.17, ...), custom_call_target="tpu_custom_call" | custom-call | tf_op jit(solution)/shard_map/pallas_call | solution.py:406
  61.1 1.7 %copy.14 = bf16[256,2,1,128]{3,1,2,0:T(2,128)(2,1)} copy(bf16[256,2,1,128]{3,1,2,0:T(2,128)(2,1)} %bitcast.11) | data formatting | bytes 262144

commit v3 on v2

--- a/solution.py
+++ b/solution.py
@@ -22,17 +22,23 @@
 NT = (((1,), (1,)), ((), ()))
 DIST = (4, 3, 5, 2, 6, 1, 7, 0)
 COLUMNS = (0, 1, -1, 2)
-GROUP = 6 * PRE
-FIRST = [(0, 0), (1, 0), (2, 0), (3, 0), (0, 1), (0, 3)]
+FIRST = [(0, 0), (1, 0), (2, 0), (3, 0), (0, 1), (0, 3), (0, 2)]
 SECOND = [(1, 1), (2, 1), (3, 1), (1, 3), (2, 3), (3, 3)]
-LAST = [(0, 2), (1, 2), (2, 2), (3, 2)]
+LAST = [(1, 2), (2, 2), (3, 2)]
+ALL = FIRST + SECOND + LAST
+SIZES = (len(FIRST) * PRE, len(SECOND) * PRE, len(ALL) * NEW, len(LAST) * PRE)
+STARTS = tuple(sum(SIZES[:k]) for k in range(4))
+FRESH = 2
+KEYS = sum(SIZES)
+KEY_AT, VALUE_AT = 2 * NEW, 2 * NEW + PRE
+HALVES = (pl.ds(0, PIECE // 2), pl.ds(PIECE // 2, PIECE // 2))
 
 
 def kernel(
     ids_ref, order_ref, q_hbm, feat_hbm, down_hbm, kup_hbm, vup_hbm, bk_hbm, bv_hbm, pk_hbm, pv_hbm,
     out_ref,
     q_ref, feat_ref, down_ref, up_ref, pre_ref, base_ref, wide, own_rows, ups, lat_part, lat_sib,
-    lat_chip, lat_team, lat_pair, lat_all, q_own, qbuf, kv, keys, values, vt, bias, scores_a, scores_b,
+    lat_chip, lat_team, lat_pair, lat_all, q_own, qbuf, kv, keys, values, vt, bias, scores,
     acc, tops, sent, from_sib, landed, local_sem, send_sem, recv_sem, core_send, core_recv, home_send, home_recv,
 ):
     team = lax.axis_index("team")
@@ -112,30 +118,55 @@
             rows = pick(pre_ref[kind], 2 * PRE)
             fresh = pick(base_ref[kind], 2 * NEW)
             for c in range(2):
-                own_rows[c, kind * PRE : (kind + 1) * PRE, :] = rows[c * PRE : (c + 1) * PRE]
-                at = 2 * PRE + kind * NEW
-                own_rows[c, at : at + NEW, :] = fresh[c * NEW : (c + 1) * NEW]
+                at = KEY_AT + kind * PRE
+                own_rows[c, at : at + PRE, :] = rows[c * PRE : (c + 1) * PRE]
+                own_rows[c, kind * NEW : (kind + 1) * NEW, :] = fresh[c * NEW : (c + 1) * NEW]
             for a in range(ADAPTERS):
                 ups[a, :, kind * HD : (kind + 1) * HD] = pick(up_ref[kind, a], RANK)
         kv[0, 0] = own_rows[core]
-        qbuf[7] = q_own[mine]
+        qbuf[3, QN:, :] = q_own[mine]
 
     pl.semaphore_wait(barrier, len(peers))
+
+    def q_slot(i):
+        return qbuf.at[i // 2, pl.ds((i % 2) * QN, QN)]
 
     lat_core = link(lat_part.at[1 - core], lat_sib, sibling)
     share_rows = link(own_rows.at[1 - core], kv.at[0, 0], sibling)
     share_ups = link(ups, ups, sibling)
-    share_q = [link(qbuf.at[i], qbuf.at[i], sibling) for i in range(TEAM)]
+    share_q = [link(q_slot(i), q_slot(i), sibling) for i in range(TEAM)]
     team_q = [
-        link(q_own.at[(team + DIST[i]) % 2], qbuf.at[i], at_z(DIST[i])) for i in range(TEAM - 1)
+        link(q_own.at[(team + DIST[i]) % 2], q_slot(i), at_z(DIST[i])) for i in range(TEAM - 1)
     ]
     takes_q = [((team + DIST[i]) % 4) // 2 == core for i in range(TEAM - 1)]
 
+    down_y = {
+        (d, h): link(kv.at[0, 0, HALVES[h]], kv.at[0, d, HALVES[h]], at_blk(d, 0))
+        for d, h in ((1, 0), (3, 0), (1, 1), (3, 1), (2, 0), (2, 1))
+    }
+    round_x = {}
+
+    def send_x(d, h):
+        if d:
+            down_y[d, h].wait_recv()
+        for c in (1, 2, 3):
+            round_x[c, d, h] = link(kv.at[0, d, HALVES[h]], kv.at[c, d, HALVES[h]], at_blk(0, COLUMNS[c]))
+            round_x[c, d, h].start()
+
+    @pl.when(is_owner)
+    def _():
+        share_rows.start()
+
     lat_core.start()
 
-    @pl.when(is_owner)
-    def _():
-        share_rows.start()
+    @pl.when(not_owner)
+    def _():
+        share_rows.wait_recv()
+
+    for copy in down_y.values():
+        copy.start()
+    send_x(0, 0)
+    send_x(0, 1)
 
     lat_core.wait_recv()
     for h in range(2):
@@ -148,24 +179,6 @@
     for i in range(TEAM - 1):
         pl.when(takes_q[i])(team_q[i].start)
 
-    @pl.when(not_owner)
-    def _():
-        share_rows.wait_recv()
-
-    down_y = {d: link(kv.at[0, 0], kv.at[0, d], at_blk(d, 0)) for d in (1, 3, 2)}
-    round_x = {}
-
-    def send_x(d):
-        if d:
-            down_y[d].wait_recv()
-        for c in (1, 2, 3):
-            round_x[c, d] = link(kv.at[0, d], kv.at[c, d], at_blk(0, COLUMNS[c]))
-            round_x[c, d].start()
-
-    for copy in down_y.values():
-        copy.start()
-    send_x(0)
-
     @pl.when(is_owner)
     def _():
         share_ups.start()
@@ -177,14 +190,15 @@
     def owner_of(column, d):
         return ((yh - d + YN) % YN) * XN + (x - COLUMNS[column] + XN) % XN
 
-    for k, (column, d) in enumerate(FIRST + SECOND + LAST):
+    for k, (column, d) in enumerate(ALL):
         hidden = order_ref[owner_of(column, d)] * QN + within > token
         bias[k * NEW : (k + 1) * NEW, :] = jnp.where(hidden, -1e30, 0.0)
-    for group in range(4):
-        vt[group, HD:MSG, :] = jnp.ones((TAIL, GROUP), BF16)
-
-    send_x(1)
-    send_x(3)
+    vt[HD:MSG, :] = jnp.ones((TAIL, KEYS), BF16)
+
+    send_x(1, 0)
+    send_x(3, 0)
+    send_x(1, 1)
+    send_x(3, 1)
 
     for copy in lat_z:
         copy.wait_recv()
@@ -209,7 +223,8 @@
     for copy in lat_blk.values():
         copy.start()
 
-    send_x(2)
+    send_x(2, 0)
+    send_x(2, 1)
 
     @pl.when(not_owner)
     def _():
@@ -217,78 +232,84 @@
             share_q[i].wait_recv()
         share_ups.wait_recv()
 
-    def put_prefix(group, at, slot):
-        keys[group, at : at + PRE, :] = kv[slot[0], slot[1], 0:PRE, :]
-        values[group, at : at + PRE, :] = kv[slot[0], slot[1], PRE : 2 * PRE, :]
-
-    def put_fresh(group, at, slot):
+    def arrived(slot, h):
+        if slot[0]:
+            round_x[slot[0], slot[1], h].wait_recv()
+
+    def put_prefix(at, slot):
+        keys[at : at + PRE, :] = kv[slot[0], slot[1], KEY_AT:VALUE_AT, :]
+        values[at : at + PRE, :] = kv[slot[0], slot[1], VALUE_AT:PIECE, :]
+
+    def put_fresh(at, slot):
         packed = lat_all[slot[0], slot[1]].astype(F32)
         latent = jnp.concatenate(
             [jnp.where(first_half, packed, 0.0), jnp.where(first_half, 0.0, packed)], axis=0
         ).astype(BF16)
         up = ups[ids_ref[owner_of(*slot)]]
         delta = jnp.dot(latent, jnp.concatenate([up, up], axis=0), preferred_element_type=F32)
-        base = kv[slot[0], slot[1], 2 * PRE : PIECE, :].astype(F32)
-        keys[group, at : at + NEW, :] = (base[0:NEW] + delta[:, 0:HD]).astype(BF16)
-        values[group, at : at + NEW, :] = (base[NEW:] + delta[:, HD:]).astype(BF16)
+        base = kv[slot[0], slot[1], 0 : 2 * NEW, :].astype(F32)
+        keys[at : at + NEW, :] = (base[0:NEW] + delta[:, 0:HD]).astype(BF16)
+        values[at : at + NEW, :] = (base[NEW:] + delta[:, HD:]).astype(BF16)
 
     def turn(group):
-        vt[group, 0:HD, :] = values[group].T
-
-    def step(group, i, scores):
-        s = lax.dot_general(keys[group], qbuf[i], NT, preferred_element_type=F32)
-        if group == 2:
-            s = s + bias[0:GROUP, :]
-        if group == 3:
-            plain = 4 * PRE
-            s = jnp.concatenate([s[0:plain], s[plain:] + bias[GROUP:, :]], axis=0)
-        scores[...] = s
-        top = jnp.max(s.reshape(GROUP // 8, 8, QN), axis=0)
+        at, size = STARTS[group], SIZES[group]
+        vt[0:HD, at : at + size] = values[at : at + size, :].T
+
+    def score(group, k):
+        at, size = STARTS[group], SIZES[group]
+        s = lax.dot_general(keys[at : at + size, :], qbuf[k], NT, preferred_element_type=F32)
+        if group == FRESH:
+            s = s + jnp.concatenate([bias[...], bias[...]], axis=1)
+        scores[k % 2, 0:size, :] = s
+        top = jnp.max(s.reshape(size // 8, 8, 2 * QN), axis=0)
         top = jnp.max(top, axis=0, keepdims=True) * LOG_SCALE
-        top = top.astype(BF16).astype(F32)
+        return top.astype(BF16).astype(F32)
+
+    def weigh(group, k, top):
+        at, size = STARTS[group], SIZES[group]
         if group:
-            before = tops[i, 0:1, :]
+            before = tops[k, 0:1, :]
             top = jnp.maximum(top, before)
-        p = jnp.exp2(scores[...] * LOG_SCALE - top).astype(BF16)
-        weighted = jnp.dot(vt[group], p, preferred_element_type=F32)
+        p = jnp.exp2(scores[k % 2, 0:size, :] * LOG_SCALE - top).astype(BF16)
+        weighted = jnp.dot(vt[:, at : at + size], p, preferred_element_type=F32)
         if group:
-            weighted = weighted + acc[i] * jnp.exp2(before - top)
-        acc[i] = weighted
-        tops[i] = jnp.broadcast_to(top, (8, QN))
-
-    def run(group):
-        def both(k, carry):
-            step(group, 2 * k, scores_a)
-            step(group, 2 * k + 1, scores_b)
-            return carry
-
-        lax.fori_loop(0, TEAM // 2, both, 0)
+            weighted = weighted + acc[k] * jnp.exp2(before - top)
+        acc[k] = weighted
+        tops[k] = jnp.broadcast_to(top, (8, 2 * QN))
+
+    def run(group, first=0, count=TEAM // 2):
+        top = score(group, first)
+        for k in range(first, first + count):
+            ahead = score(group, k + 1) if k + 1 < first + count else None
+            weigh(group, k, top)
+            top = ahead
 
     for k, slot in enumerate(FIRST):
-        if slot[0]:
-            round_x[slot].wait_recv()
-        put_prefix(0, k * PRE, slot)
+        for h in range(2):
+            arrived(slot, h)
+        put_prefix(STARTS[0] + k * PRE, slot)
     turn(0)
     run(0)
 
     for k, slot in enumerate(SECOND):
-        round_x[slot].wait_recv()
-        put_prefix(1, k * PRE, slot)
+        for h in range(2):
+            arrived(slot, h)
+        put_prefix(STARTS[1] + k * PRE, slot)
     turn(1)
     run(1)
 
     for copy in lat_blk.values():
         copy.wait_recv()
-    for k, slot in enumerate(FIRST + SECOND):
-        put_fresh(2, k * NEW, slot)
-    turn(2)
-    run(2)
+    for slot in LAST:
+        arrived(slot, 0)
+    for k, slot in enumerate(ALL):
+        put_fresh(STARTS[FRESH] + k * NEW, slot)
+    turn(FRESH)
+    run(FRESH)
 
     for k, slot in enumerate(LAST):
-        if slot[0]:
-            round_x[slot].wait_recv()
-        put_prefix(3, k * PRE, slot)
-        put_fresh(3, 4 * PRE + k * NEW, slot)
+        arrived(slot, 1)
+        put_prefix(STARTS[3] + k * PRE, slot)
     turn(3)
 
     tail_row = lax.broadcasted_iota(jnp.int32, (TAIL, QN), 0)
@@ -301,7 +322,8 @@
         ref[HD:MSG, :] = tail.astype(BF16)
 
     def held(i):
-        return acc[i, 0:HD, :], acc[i, HD : HD + 1, :], tops[i, 0:1, :]
+        side = slice((i % 2) * QN, (i % 2 + 1) * QN)
+        return acc[i // 2, 0:HD, side], acc[i // 2, HD : HD + 1, side], tops[i // 2, 0:1, side]
 
     def read(ref):
         tail = ref[HD:MSG, :].astype(F32)
@@ -332,30 +354,23 @@
         store(sent.at[i], merged(held(i), read(from_sib.at[i])))
         homeward(i, home_slot).start()
 
-    def final(k, carry):
-        step(3, 2 * k, scores_a)
-        step(3, 2 * k + 1, scores_b)
+    for stage in range(2):
+        run(3, 2 * stage, 2)
 
         @pl.when(not_owner)
         def _():
-            for i in (2 * k, 2 * k + 1):
+            for i in range(4 * stage, 4 * stage + 4):
                 store(sent.at[i], held(i))
                 to_sibling(i).start()
 
-        @pl.when(jnp.logical_and(is_owner, k > 0))
-        def _():
-            for i in (2 * k - 2, 2 * k - 1):
-                merge_and_send(i)
-
-        return carry
-
-    lax.fori_loop(0, TEAM // 2, final, 0)
-
-    @pl.when(is_owner)
-    def _():
-        merge_and_send(6)
-        to_sibling(7).wait_recv()
-        store(landed.at[home_slot], merged(held(7), read(from_sib.at[7])))
+        if stage:
+
+            @pl.when(is_owner)
+            def _():
+                for i in range(TEAM - 1):
+                    merge_and_send(i)
+                to_sibling(7).wait_recv()
+                store(landed.at[home_slot], merged(held(7), read(from_sib.at[7])))
 
     for h in range(KV):
         for part in range(2):
@@ -398,7 +413,7 @@
     queries, features, adapter_down, adapter_key_up, adapter_value_up,
     base_key, base_value, prefix_key, prefix_value, adapter_ids, block_order,
 ):
-    copies = 1 + 1 + 1 + 8 + 7 + 7 + 1 + 15 + 3 + 12
+    copies = 1 + 1 + 1 + 8 + 7 + 7 + 1 + 15 + 6 + 24
     vmem = pl.BlockSpec(memory_space=pltpu.VMEM)
     smem = pl.BlockSpec(memory_space=pltpu.SMEM)
     hbm = pl.BlockSpec(memory_space=pl.ANY)
@@ -425,16 +440,15 @@
             pltpu.VMEM((2, 32, HD), F32),
             pltpu.VMEM((XN, YN, 32, HD), BF16),
             pltpu.VMEM((KV, QN, HD), BF16),
-            pltpu.VMEM((TEAM, QN, HD), BF16),
+            pltpu.VMEM((TEAM // 2, 2 * QN, HD), BF16),
             pltpu.VMEM((XN, YN, PIECE, HD), BF16),
-            pltpu.VMEM((4, GROUP, HD), BF16),
-            pltpu.VMEM((4, GROUP, HD), BF16),
-            pltpu.VMEM((4, MSG, GROUP), BF16),
+            pltpu.VMEM((KEYS, HD), BF16),
+            pltpu.VMEM((KEYS, HD), BF16),
+            pltpu.VMEM((MSG, KEYS), BF16),
             pltpu.VMEM((XN * YN * NEW, QN), F32),
-            pltpu.VMEM((GROUP, QN), F32),
-            pltpu.VMEM((GROUP, QN), F32),
-            pltpu.VMEM((TEAM, MSG, QN), F32),
-            pltpu.VMEM((TEAM, 8, QN), F32),
+            pltpu.VMEM((2, max(SIZES), 2 * QN), F32),
+            pltpu.VMEM((TEAM // 2, MSG, 2 * QN), F32),
+            pltpu.VMEM((TEAM // 2, 8, 2 * QN), F32),
             pltpu.VMEM((TEAM, MSG, QN), BF16),
             pltpu.VMEM((TEAM, MSG, QN), BF16),
             pltpu.VMEM((4, MSG, QN), BF16),

time: 63 us -> 54.9 us (0.87)
  Pallas kernels: 61.1 us -> 53 us
    pallas_call x1, Pallas kernels: 61.1 us -> 53 us  [on_device(): pl.pallas_call(kernel, out_shape=jax.ShapeDtypeStruct((KV * QN, HD), BF16...]
where the time goes in v3:
time: 54.9 us; the launch traced here: 54.7 us
  Pallas kernels  53 us (97%)
  local copies, waits for them, and re-layouts  1.65 us (3%)
    pallas_call x1, Pallas kernels, on_device(): pl.pallas_call(kernel, out_shape=jax.ShapeDtypeStruct((KV * QN, HD), BF16...  53 us
    unnamed x1, local copies, waits for them, and re-layouts  1.65 us

profile of v3, /device:TPU:1, one launch (start us, length us, event | category | flops | bytes accessed | tf_op | source)
XLA Modules:
  0.0 54.7 jit_solution(8076550040599951015)
XLA Ops:
  0.0 53.0 %shard_map.109 = bf16[512,128]{1,0:T(8,128)(2,1)} custom-call(s32[16]{0:T(128)} %ids_ref.1, s32[16]{0:T(128)} %order_ref.1, bf16[512,128]{1,0:T(8,128)(2,1)} %bitcast.14, bf16[256,256]{1,0:T(8,128)(2,1)} %feat_hbm.1, bf16[4,64,256]{2,1,0:T(8,128)(2,1)} %bitcast.15, bf16[4,128,128]{2,1,0:T(8,128)(2,1)} %bitcast.16, bf16[4,128,128]{2,1,0:T(8,128)(2,1)} %bitcast.17, ...), custom_call_target="tpu_custom_call" | custom-call | tf_op jit(solution)/shard_map/pallas_call | solution.py:421
  53.1 1.7 %copy.14 = bf16[256,2,1,128]{3,1,2,0:T(2,128)(2,1)} copy(bf16[256,2,1,128]{3,1,2,0:T(2,128)(2,1)} %bitcast.11) | data formatting | bytes 262144

commit v4 on v3

--- a/solution.py
+++ b/solution.py
@@ -26,19 +26,25 @@
 SECOND = [(1, 1), (2, 1), (3, 1), (1, 3), (2, 3), (3, 3)]
 LAST = [(1, 2), (2, 2), (3, 2)]
 ALL = FIRST + SECOND + LAST
-SIZES = (len(FIRST) * PRE, len(SECOND) * PRE, len(ALL) * NEW, len(LAST) * PRE)
-STARTS = tuple(sum(SIZES[:k]) for k in range(4))
-FRESH = 2
+HALF = PRE // 2
+EARLY = 12
+SIZES = (
+    len(FIRST) * PRE, len(SECOND) * HALF, len(SECOND) * HALF, EARLY * NEW,
+    len(LAST) * PRE + (len(ALL) - EARLY) * NEW,
+)
+STARTS = tuple(sum(SIZES[:k]) for k in range(5))
 KEYS = sum(SIZES)
-KEY_AT, VALUE_AT = 2 * NEW, 2 * NEW + PRE
-HALVES = (pl.ds(0, PIECE // 2), pl.ds(PIECE // 2, PIECE // 2))
+NEW_KEY, NEW_VALUE = 0, 2 * HALF + NEW
+PREFIX_AT = (NEW, 2 * NEW + 2 * HALF)
+CUT = PREFIX_AT[1] - NEW // 2
+PARTS = (pl.ds(0, CUT), pl.ds(CUT, PIECE - CUT))
 
 
 def kernel(
     ids_ref, order_ref, q_hbm, feat_hbm, down_hbm, kup_hbm, vup_hbm, bk_hbm, bv_hbm, pk_hbm, pv_hbm,
     out_ref,
     q_ref, feat_ref, down_ref, up_ref, pre_ref, base_ref, wide, own_rows, ups, lat_part, lat_sib,
-    lat_chip, lat_team, lat_pair, lat_all, q_own, qbuf, kv, keys, values, vt, bias, scores,
+    lat_chip, lat_send, lat_team, lat_pair, lat_all, q_own, qbuf, kv, keys, values, vt, bias, scores,
     acc, tops, sent, from_sib, landed, local_sem, send_sem, recv_sem, core_send, core_recv, home_send, home_recv,
 ):
     team = lax.axis_index("team")
@@ -59,10 +65,11 @@
     sibling = {"head": ylo * 2 + 1 - core}
     beside = {"head": (1 - ylo) * 2 + core}
     others = [(d, c) for d in range(YN) for c in range(XN) if (d, c) != (0, 0)]
+    others.sort(key=lambda dc: -2 * min(dc[0], YN - dc[0]) - abs(COLUMNS[dc[1]]))
 
     barrier = pltpu.get_barrier_semaphore()
-    peers = [at_z(d) for d in range(1, TEAM)] + [sibling, beside]
-    peers += [at_blk(d, COLUMNS[c]) for d, c in others]
+    by_z, by_blk = [at_z(d) for d in DIST[:-1]], [at_blk(d, COLUMNS[c]) for d, c in others]
+    peers = by_blk[:4] + by_z[:3] + by_blk[4:10] + by_z[3:5] + by_blk[10:] + by_z[5:] + [beside, sibling]
     for peer in peers:
         pl.semaphore_signal(barrier, inc=1, device_id=peer, device_id_type=MESH)
 
@@ -118,9 +125,12 @@
             rows = pick(pre_ref[kind], 2 * PRE)
             fresh = pick(base_ref[kind], 2 * NEW)
             for c in range(2):
-                at = KEY_AT + kind * PRE
-                own_rows[c, at : at + PRE, :] = rows[c * PRE : (c + 1) * PRE]
-                own_rows[c, kind * NEW : (kind + 1) * NEW, :] = fresh[c * NEW : (c + 1) * NEW]
+                at = NEW_VALUE if kind else NEW_KEY
+                own_rows[c, at : at + NEW, :] = fresh[c * NEW : (c + 1) * NEW]
+                for h in range(2):
+                    at = PREFIX_AT[h] + kind * HALF
+                    row = c * PRE + h * HALF
+                    own_rows[c, at : at + HALF, :] = rows[row : row + HALF]
             for a in range(ADAPTERS):
                 ups[a, :, kind * HD : (kind + 1) * HD] = pick(up_ref[kind, a], RANK)
         kv[0, 0] = own_rows[core]
@@ -140,43 +150,54 @@
     ]
     takes_q = [((team + DIST[i]) % 4) // 2 == core for i in range(TEAM - 1)]
 
-    down_y = {
-        (d, h): link(kv.at[0, 0, HALVES[h]], kv.at[0, d, HALVES[h]], at_blk(d, 0))
-        for d, h in ((1, 0), (3, 0), (1, 1), (3, 1), (2, 0), (2, 1))
-    }
-    round_x = {}
-
-    def send_x(d, h):
+    def rows_at(column, d, part):
+        return kv.at[column, d, PARTS[part]]
+
+    def along_y(column, d, part):
+        copy = link(rows_at(column, 0, part), rows_at(column, d, part), at_blk(d, 0))
+        copy.start()
+        return copy
+
+    def along_x(column, d, part):
+        copy = link(rows_at(0, d, part), rows_at(column, d, part), at_blk(0, COLUMNS[column]))
+        copy.start()
+        return copy
+
+    moved = {}
+
+    def send_x(d, part):
         if d:
-            down_y[d, h].wait_recv()
-        for c in (1, 2, 3):
-            round_x[c, d, h] = link(kv.at[0, d, HALVES[h]], kv.at[c, d, HALVES[h]], at_blk(0, COLUMNS[c]))
-            round_x[c, d, h].start()
+            moved[0, d, part].wait_recv()
+        for c in (3, 1, 2):
+            moved[c, d, part] = along_x(c, d, part)
 
     @pl.when(is_owner)
     def _():
         share_rows.start()
 
     lat_core.start()
+    pl.when(takes_q[0])(team_q[0].start)
 
     @pl.when(not_owner)
     def _():
         share_rows.wait_recv()
 
-    for copy in down_y.values():
-        copy.start()
+    for d, part in ((1, 0), (3, 0), (1, 1), (3, 1), (2, 0), (2, 1)):
+        moved[0, d, part] = along_y(0, d, part)
     send_x(0, 0)
     send_x(0, 1)
 
     lat_core.wait_recv()
     for h in range(2):
-        lat_chip[h] = lat_part[core, h] + lat_sib[h]
+        total = lat_part[core, h] + lat_sib[h]
+        lat_chip[h] = total
+        lat_send[h] = total.astype(BF16)
     lat_z = [
-        link(lat_chip.at[((team + d) % TEAM) // 4], lat_team.at[d], at_z(d)) for d in range(1, TEAM)
+        link(lat_send.at[((team + d) % TEAM) // 4], lat_team.at[d], at_z(d)) for d in DIST[:-1]
     ]
     for copy in lat_z:
         copy.start()
-    for i in range(TEAM - 1):
+    for i in range(1, TEAM - 1):
         pl.when(takes_q[i])(team_q[i].start)
 
     @pl.when(is_owner)
@@ -204,17 +225,12 @@
         copy.wait_recv()
     total = lat_chip[half]
     for d in range(1, TEAM):
-        total = total + lat_team[d]
+        total = total + lat_team[d].astype(F32)
     lat_pair[0] = total
     lat_y = link(lat_pair.at[0], lat_pair.at[1], beside)
     lat_y.start()
 
-    @pl.when(is_owner)
-    def _():
-        for i in (5, 6, 3, 4, 1, 2, 0):
-            team_q[i].wait_recv()
-            share_q[i].start()
-
+    send_x(2, 0)
     lat_y.wait_recv()
     lat_all[0, 0] = (lat_pair[0] + lat_pair[1]).astype(BF16)
     lat_blk = {
@@ -223,8 +239,13 @@
     for copy in lat_blk.values():
         copy.start()
 
-    send_x(2, 0)
     send_x(2, 1)
+
+    @pl.when(is_owner)
+    def _():
+        for i in (5, 6, 3, 4, 1, 2, 0):
+            team_q[i].wait_recv()
+            share_q[i].start()
 
     @pl.when(not_owner)
     def _():
@@ -232,13 +253,21 @@
             share_q[i].wait_recv()
         share_ups.wait_recv()
 
-    def arrived(slot, h):
-        if slot[0]:
-            round_x[slot[0], slot[1], h].wait_recv()
-
-    def put_prefix(at, slot):
-        keys[at : at + PRE, :] = kv[slot[0], slot[1], KEY_AT:VALUE_AT, :]
-        values[at : at + PRE, :] = kv[slot[0], slot[1], VALUE_AT:PIECE, :]
+    def arrived(slots, part):
+        for column, d in slots:
+            pending = (column, d, part) in moved and (column, d, part) not in waited
+            if pending:
+                waited.add((column, d, part))
+                moved[column, d, part].wait_recv()
+
+    waited = {(0, d, part) for d in (1, 2, 3) for part in (0, 1)}
+
+    def put_prefix(at, slots, part):
+        row = PREFIX_AT[part]
+        for k, (column, d) in enumerate(slots):
+            to = at + k * HALF
+            keys[to : to + HALF, :] = kv[column, d, row : row + HALF, :]
+            values[to : to + HALF, :] = kv[column, d, row + HALF : row + 2 * HALF, :]
 
     def put_fresh(at, slot):
         packed = lat_all[slot[0], slot[1]].astype(F32)
@@ -247,9 +276,10 @@
         ).astype(BF16)
         up = ups[ids_ref[owner_of(*slot)]]
         delta = jnp.dot(latent, jnp.concatenate([up, up], axis=0), preferred_element_type=F32)
-        base = kv[slot[0], slot[1], 0 : 2 * NEW, :].astype(F32)
-        keys[at : at + NEW, :] = (base[0:NEW] + delta[:, 0:HD]).astype(BF16)
-        values[at : at + NEW, :] = (base[NEW:] + delta[:, HD:]).astype(BF16)
+        new_key = kv[slot[0], slot[1], NEW_KEY : NEW_KEY + NEW, :].astype(F32)
+        new_value = kv[slot[0], slot[1], NEW_VALUE : NEW_VALUE + NEW, :].astype(F32)
+        keys[at : at + NEW, :] = (new_key + delta[:, 0:HD]).astype(BF16)
+        values[at : at + NEW, :] = (new_value + delta[:, HD:]).astype(BF16)
 
     def turn(group):
         at, size = STARTS[group], SIZES[group]
@@ -258,8 +288,11 @@
     def score(group, k):
         at, size = STARTS[group], SIZES[group]
         s = lax.dot_general(keys[at : at + size, :], qbuf[k], NT, preferred_element_type=F32)
-        if group == FRESH:
-            s = s + jnp.concatenate([bias[...], bias[...]], axis=1)
+        first = 0 if group == 3 else len(LAST) * PRE if group == 4 else size
+        if first < size:
+            hide = bias[(0 if group == 3 else EARLY * NEW) :, :][: size - first]
+            hide = s[first:] + jnp.concatenate([hide, hide], axis=1)
+            s = jnp.concatenate([s[:first], hide], axis=0) if first else hide
         scores[k % 2, 0:size, :] = s
         top = jnp.max(s.reshape(size // 8, 8, 2 * QN), axis=0)
         top = jnp.max(top, axis=0, keepdims=True) * LOG_SCALE
@@ -277,40 +310,39 @@
         acc[k] = weighted
         tops[k] = jnp.broadcast_to(top, (8, 2 * QN))
 
-    def run(group, first=0, count=TEAM // 2):
-        top = score(group, first)
-        for k in range(first, first + count):
-            ahead = score(group, k + 1) if k + 1 < first + count else None
+    def run(group):
+        top = score(group, 0)
+        for k in range(TEAM // 2):
+            ahead = score(group, k + 1) if k + 1 < TEAM // 2 else None
             weigh(group, k, top)
             top = ahead
 
-    for k, slot in enumerate(FIRST):
-        for h in range(2):
-            arrived(slot, h)
-        put_prefix(STARTS[0] + k * PRE, slot)
+    for part in range(2):
+        arrived(FIRST, part)
+        put_prefix(STARTS[0] + part * len(FIRST) * HALF, FIRST, part)
     turn(0)
     run(0)
 
-    for k, slot in enumerate(SECOND):
-        for h in range(2):
-            arrived(slot, h)
-        put_prefix(STARTS[1] + k * PRE, slot)
-    turn(1)
-    run(1)
+    for part in range(2):
+        arrived(SECOND, part)
+        put_prefix(STARTS[1 + part], SECOND, part)
+        turn(1 + part)
+        run(1 + part)
 
     for copy in lat_blk.values():
         copy.wait_recv()
-    for slot in LAST:
-        arrived(slot, 0)
-    for k, slot in enumerate(ALL):
-        put_fresh(STARTS[FRESH] + k * NEW, slot)
-    turn(FRESH)
-    run(FRESH)
-
-    for k, slot in enumerate(LAST):
-        arrived(slot, 1)
-        put_prefix(STARTS[3] + k * PRE, slot)
+    for k, slot in enumerate(ALL[:EARLY]):
+        put_fresh(STARTS[3] + k * NEW, slot)
     turn(3)
+    run(3)
+
+    for part in range(2):
+        arrived(ALL[EARLY:], part)
+    for part in range(2):
+        put_prefix(STARTS[4] + part * len(LAST) * HALF, LAST, part)
+    for k, slot in enumerate(ALL[EARLY:]):
+        put_fresh(STARTS[4] + len(LAST) * PRE + k * NEW, slot)
+    turn(4)
 
     tail_row = lax.broadcasted_iota(jnp.int32, (TAIL, QN), 0)
 
@@ -354,23 +386,30 @@
         store(sent.at[i], merged(held(i), read(from_sib.at[i])))
         homeward(i, home_slot).start()
 
-    for stage in range(2):
-        run(3, 2 * stage, 2)
+    top = score(4, 0)
+    for k in range(TEAM // 2):
+        ahead = score(4, k + 1) if k + 1 < TEAM // 2 else None
+        weigh(4, k, top)
+        top = ahead
 
         @pl.when(not_owner)
         def _():
-            for i in range(4 * stage, 4 * stage + 4):
+            for i in (2 * k, 2 * k + 1):
                 store(sent.at[i], held(i))
                 to_sibling(i).start()
 
-        if stage:
+        if k:
 
             @pl.when(is_owner)
             def _():
-                for i in range(TEAM - 1):
-                    merge_and_send(i)
-                to_sibling(7).wait_recv()
-                store(landed.at[home_slot], merged(held(7), read(from_sib.at[7])))
+                merge_and_send(2 * k - 2)
+                merge_and_send(2 * k - 1)
+
+    @pl.when(is_owner)
+    def _():
+        merge_and_send(6)
+        to_sibling(7).wait_recv()
+        store(landed.at[home_slot], merged(held(7), read(from_sib.at[7])))
 
     for h in range(KV):
         for part in range(2):
@@ -384,7 +423,7 @@
         wide[pl.ds(h, QN, stride=2), :] = (weighted / row_sum).T
     out_ref[...] = wide[0 : KV * QN, :].astype(BF16)
 
-    for copy in [lat_core, lat_y, *lat_z, *down_y.values(), *round_x.values(), *lat_blk.values()]:
+    for copy in [lat_core, lat_y, *lat_z, *moved.values(), *lat_blk.values()]:
         copy.wait_send()
     for i in range(TEAM - 1):
         pl.when(takes_q[i])(team_q[i].wait_send)
@@ -413,7 +452,7 @@
     queries, features, adapter_down, adapter_key_up, adapter_value_up,
     base_key, base_value, prefix_key, prefix_value, adapter_ids, block_order,
 ):
-    copies = 1 + 1 + 1 + 8 + 7 + 7 + 1 + 15 + 6 + 24
+    copies = 1 + 1 + 1 + 8 + 7 + 7 + 1 + 15 + 30
     vmem = pl.BlockSpec(memory_space=pltpu.VMEM)
     smem = pl.BlockSpec(memory_space=pltpu.SMEM)
     hbm = pl.BlockSpec(memory_space=pl.ANY)
@@ -436,7 +475,8 @@
             pltpu.VMEM((2, 2, 32, HD), F32),
             pltpu.VMEM((2, 32, HD), F32),
             pltpu.VMEM((2, 32, HD), F32),
-            pltpu.VMEM((TEAM, 32, HD), F32),
+            pltpu.VMEM((2, 32, HD), BF16),
+            pltpu.VMEM((TEAM, 32, HD), BF16),
             pltpu.VMEM((2, 32, HD), F32),
             pltpu.VMEM((XN, YN, 32, HD), BF16),
             pltpu.VMEM((KV, QN, HD), BF16),

time: 54.9 us -> 54.4 us (level)
  no operation moved by 1% of the time
where the time goes in v4:
time: 54.4 us; the launch traced here: 54.2 us
  Pallas kernels  52.5 us (97%)
  local copies, waits for them, and re-layouts  1.65 us (3%)
    pallas_call x1, Pallas kernels, on_device(): pl.pallas_call(kernel, out_shape=jax.ShapeDtypeStruct((KV * QN, HD), BF16...  52.5 us
    unnamed x1, local copies, waits for them, and re-layouts  1.65 us

profile of v4, /device:TPU:1, one launch (start us, length us, event | category | flops | bytes accessed | tf_op | source)
XLA Modules:
  0.0 54.2 jit_solution(3248338999412200994)
XLA Ops:
  0.0 52.5 %shard_map.109 = bf16[512,128]{1,0:T(8,128)(2,1)} custom-call(s32[16]{0:T(128)} %ids_ref.1, s32[16]{0:T(128)} %order_ref.1, bf16[512,128]{1,0:T(8,128)(2,1)} %bitcast.14, bf16[256,256]{1,0:T(8,128)(2,1)} %feat_hbm.1, bf16[4,64,256]{2,1,0:T(8,128)(2,1)} %bitcast.15, bf16[4,128,128]{2,1,0:T(8,128)(2,1)} %bitcast.16, bf16[4,128,128]{2,1,0:T(8,128)(2,1)} %bitcast.17, ...), custom_call_target="tpu_custom_call" | custom-call | tf_op jit(solution)/shard_map/pallas_call | solution.py:460
  52.6 1.7 %copy.14 = bf16[256,2,1,128]{3,1,2,0:T(2,128)(2,1)} copy(bf16[256,2,1,128]{3,1,2,0:T(2,128)(2,1)} %bitcast.11) | data formatting | bytes 262144

commit v5 on v4

--- a/solution.py
+++ b/solution.py
@@ -44,7 +44,7 @@
     ids_ref, order_ref, q_hbm, feat_hbm, down_hbm, kup_hbm, vup_hbm, bk_hbm, bv_hbm, pk_hbm, pv_hbm,
     out_ref,
     q_ref, feat_ref, down_ref, up_ref, pre_ref, base_ref, wide, own_rows, ups, lat_part, lat_sib,
-    lat_chip, lat_send, lat_team, lat_pair, lat_all, q_own, qbuf, kv, keys, values, vt, bias, scores,
+    lat_chip, lat_team, lat_pair, lat_all, q_own, qbuf, kv, keys, values, vt, bias, scores,
     acc, tops, sent, from_sib, landed, local_sem, send_sem, recv_sem, core_send, core_recv, home_send, home_recv,
 ):
     team = lax.axis_index("team")
@@ -189,11 +189,9 @@
 
     lat_core.wait_recv()
     for h in range(2):
-        total = lat_part[core, h] + lat_sib[h]
-        lat_chip[h] = total
-        lat_send[h] = total.astype(BF16)
+        lat_chip[h] = lat_part[core, h] + lat_sib[h]
     lat_z = [
-        link(lat_send.at[((team + d) % TEAM) // 4], lat_team.at[d], at_z(d)) for d in DIST[:-1]
+        link(lat_chip.at[((team + d) % TEAM) // 4], lat_team.at[d], at_z(d)) for d in DIST[:-1]
     ]
     for copy in lat_z:
         copy.start()
@@ -225,7 +223,7 @@
         copy.wait_recv()
     total = lat_chip[half]
     for d in range(1, TEAM):
-        total = total + lat_team[d].astype(F32)
+        total = total + lat_team[d]
     lat_pair[0] = total
     lat_y = link(lat_pair.at[0], lat_pair.at[1], beside)
     lat_y.start()
@@ -475,8 +473,7 @@
             pltpu.VMEM((2, 2, 32, HD), F32),
             pltpu.VMEM((2, 32, HD), F32),
             pltpu.VMEM((2, 32, HD), F32),
-            pltpu.VMEM((2, 32, HD), BF16),
-            pltpu.VMEM((TEAM, 32, HD), BF16),
+            pltpu.VMEM((TEAM, 32, HD), F32),
             pltpu.VMEM((2, 32, HD), F32),
             pltpu.VMEM((XN, YN, 32, HD), BF16),
             pltpu.VMEM((KV, QN, HD), BF16),

time: 54.4 us -> 54.4 us (level)
  no operation moved by 1% of the time
where the time goes in v5:
time: 54.4 us; the launch traced here: 54.3 us
  Pallas kernels  52.6 us (97%)
  local copies, waits for them, and re-layouts  1.65 us (3%)
    pallas_call x1, Pallas kernels, on_device(): pl.pallas_call(kernel, out_shape=jax.ShapeDtypeStruct((KV * QN, HD), BF16...  52.6 us
    unnamed x1, local copies, waits for them, and re-layouts  1.65 us

profile of v5, /device:TPU:1, one launch (start us, length us, event | category | flops | bytes accessed | tf_op | source)
XLA Modules:
  0.0 54.3 jit_solution(16077206477760154538)
XLA Ops:
  0.0 52.6 %shard_map.109 = bf16[512,128]{1,0:T(8,128)(2,1)} custom-call(s32[16]{0:T(128)} %ids_ref.1, s32[16]{0:T(128)} %order_ref.1, bf16[512,128]{1,0:T(8,128)(2,1)} %bitcast.14, bf16[256,256]{1,0:T(8,128)(2,1)} %feat_hbm.1, bf16[4,64,256]{2,1,0:T(8,128)(2,1)} %bitcast.15, bf16[4,128,128]{2,1,0:T(8,128)(2,1)} %bitcast.16, bf16[4,128,128]{2,1,0:T(8,128)(2,1)} %bitcast.17, ...), custom_call_target="tpu_custom_call" | custom-call | tf_op jit(solution)/shard_map/pallas_call | solution.py:458
  52.6 1.7 %copy.14 = bf16[256,2,1,128]{3,1,2,0:T(2,128)(2,1)} copy(bf16[256,2,1,128]{3,1,2,0:T(2,128)(2,1)} %bitcast.11) | data formatting | bytes 262144
